TPU v7x, 32 devices: a whole 2x2x4 slice. The times are simulated.
32 devices in a mesh: gene: 4 (over y, x), bin: 8 (over z, core).
Axes of the slice: x: 2, y: 2, z: 4, core: 2. Of those that a mesh axis runs over, the one named last changes fastest.
Arguments:
- counts: bfloat16 [24576, 18432], P('bin', 'gene'), may hold values from 2 to 80
- factors: float32 [24576, 256], P('bin'), may hold values from 0.01 to 1
- loadings: float32 [256, 18432], P(None, 'gene'), may hold values from 0.01 to 1
- position: int32 [24576], P('bin'), may hold values from 0 to 24575, as said below
- edge_codes: int32 [96, 256], P('bin'), may hold values from 1 to 15
Outputs:
- factors_new: float32 [24576, 256], P('bin')
- loadings_new: float32 [256, 18432], P(None, 'gene')
Inputs may be any that keep to these rules, and one draw needn't show every extreme that they name: Each grid position is named by exactly one barcode. The barcodes of one index s of bin (rows s * 3072 on) fall in 8 aligned groups of 384; group t holds positions in grid rows t * 12 to (t + 1) * 12 - 1, 384 from every such index.
All inputs are finite; a program needn't handle non-finite values.
Results may differ from a plain program's by a relative error of at most 0.0003.
Values sent between devices are 32-bit elements; how exact they have to be, the bound alone decides.
No kernel may reach another device: no remote copies, remote signals or barrier semaphores. Data moves between devices by JAX's collectives and lax.ppermute only.
A program may use at most 128 MiB of HBM per device.

v0:
```python
import jax
import jax.numpy as jnp
from jax import lax
from jax.sharding import PartitionSpec as P

K = 256
G = 18432


def passed_along(block, axis, distance):
    devices = range(lax.axis_size(axis))
    route = [(i - distance, i) for i in devices if i - distance in devices]
    return lax.ppermute(block, axis, route)


def neighbour_sum(values, from_above, from_below):
    upper = jnp.concatenate([from_above[None], values[:-1]], 0)
    lower = jnp.concatenate([values[1:], from_below[None]], 0)
    beside = jnp.pad(values[:, 1:], ((0, 0), (0, 1), (0, 0))) + jnp.pad(
        values[:, :-1], ((0, 0), (1, 0), (0, 0))
    )
    return beside + 0.5 * (lower + upper)


def neighbour_first(values, from_above, from_below):
    upper = jnp.concatenate([from_above[:, None], values[:, :-1]], 1)
    lower = jnp.concatenate([values[:, 1:], from_below[:, None]], 1)
    beside = jnp.pad(values[:, :, 1:], ((0, 0), (0, 0), (0, 1))) + jnp.pad(
        values[:, :, :-1], ((0, 0), (0, 0), (1, 0))
    )
    return beside + 0.5 * (lower + upper)


def stencil_term(payload, col_width, position, edge_codes):
    bin_count = lax.axis_size("bin")
    row_count = position.shape[0]
    group_size = row_count // bin_count
    grid_rows, grid_cols = edge_codes.shape
    pos_float = position.astype(jnp.float32).reshape(bin_count, group_size)
    got_rows, got_pos = (
        lax.all_to_all(payload, "bin", split_axis=0, concat_axis=0, tiled=True),
        lax.all_to_all(pos_float, "bin", split_axis=0, concat_axis=0, tiled=True),
    )
    tile_slot = got_pos.reshape(row_count).astype(jnp.int32) - lax.axis_index("bin") * row_count
    cell_scale = edge_codes.astype(jnp.float32) / 8.0
    tile_rows = (
        jnp.zeros((row_count, col_width), jnp.float32)
        .at[tile_slot]
        .set(got_rows.reshape(row_count, col_width))
    )
    weighted = cell_scale[:, :, None] * tile_rows.reshape(grid_rows, grid_cols, col_width)
    rim_last, rim_first = (weighted[-1], weighted[0])
    upper_rows, upper_scale = passed_along((rim_last, cell_scale[-1]), "bin", 1)
    lower_rows, lower_scale = passed_along((rim_first, cell_scale[0]), "bin", -1)
    degree_grid = (
        cell_scale * neighbour_first(cell_scale[None], upper_scale[None], lower_scale[None])[0]
    )
    back_degree = degree_grid.reshape(row_count)[tile_slot]
    smooth_grid = cell_scale[:, :, None] * neighbour_sum(weighted, upper_rows, lower_rows)
    back_send = smooth_grid.reshape(row_count, col_width)[tile_slot].reshape(
        bin_count, group_size * col_width
    )
    smooth, degree = (
        lax.all_to_all(back_send, "bin", split_axis=0, concat_axis=0, tiled=True),
        lax.all_to_all(
            back_degree.reshape(bin_count, group_size),
            "bin",
            split_axis=0,
            concat_axis=0,
            tiled=True,
        ),
    )
    smooth = smooth.reshape(row_count, col_width)
    return (smooth, degree.reshape(row_count))


def on_device(counts, factors, loadings, position, edge_codes):
    bin_count = lax.axis_size("bin")
    row_count, width_all = factors.shape
    group_size = row_count // bin_count
    load_bf = loadings.astype(jnp.bfloat16)
    right_dims = (((1,), (1,)), ((), ()))
    load_gram = lax.psum(
        lax.dot_general(load_bf, load_bf, right_dims, preferred_element_type=jnp.float32), "gene"
    )
    payload = factors.reshape(bin_count, group_size * width_all)
    smooth, degree = stencil_term(payload, width_all, position, edge_codes)
    penalty = float(G * K) / 64.0
    numer = lax.psum(
        lax.dot_general(counts, load_bf, right_dims, preferred_element_type=jnp.float32), "gene"
    )
    denom = (
        jnp.dot(factors, load_gram, precision=lax.Precision.HIGHEST)
        + penalty * degree[:, None] * factors
    )
    factors_new = factors * (numer + penalty * smooth) / denom
    fac_bf = factors_new.astype(jnp.bfloat16)
    left_dims = (((0,), (0,)), ((), ()))
    cross_part = lax.dot_general(fac_bf, counts, left_dims, preferred_element_type=jnp.float32)
    gram_part = lax.dot_general(fac_bf, fac_bf, left_dims, preferred_element_type=jnp.float32)
    cross, fac_gram = lax.psum((cross_part, gram_part), "bin")
    loadings_new = loadings * cross / jnp.dot(fac_gram, loadings, precision=lax.Precision.HIGHEST)
    return (factors_new, loadings_new)


def solution(mesh):
    placed = (P("bin", "gene"), P("bin", None), P(None, "gene"), P("bin"), P("bin", None))
    return jax.shard_map(
        on_device,
        mesh=mesh,
        in_specs=placed,
        out_specs=(P("bin", None), P(None, "gene")),
        check_vma=False,
    )
```

profile of v0, /device:TPU:0, one launch (start us, length us, event | category | flops | bytes accessed | tf_op | source)
XLA Modules:
  0.0 466.0 jit_solution(9078250100529142901)
XLA Ops:
  7.2 1.3 convert_element_type.33
  8.5 6.3 %all-to-all-start = ((f32[8,1,384]{2,1,0:T(1,128)}), f32[8,1,384]{2,1,0:T(1,128)S(1)}, u32[]{:S(2)}, u32[]{:S(2)}) async-start(f32[8,1,384]{2,1,0:T(1,128)} %bitcast), calls=%async_computation | async-start | bytes 24576 | tf_op jit(solution)/shard_map/all_to_all | solution.py:42
  14.8 7.5 %all_to_all.26 = f32[8,1,98304]{2,1,0:T(1,128)} reshape(f32[3072,256]{1,0:T(8,128)} %param.6) | data formatting | bytes 6291456 | tf_op jit(solution)/shard_map/all_to_all | solution.py:41
  22.3 0.0 all-to-all-done
  22.3 5.2 %all-to-all-start.1 = ((f32[8,1,98304]{2,1,0:T(1,128)}), f32[8,1,98304]{2,1,0:T(1,128)S(1)}, u32[]{:S(2)}, u32[]{:S(2)}) async-start(f32[8,1,98304]{2,1,0:T(1,128)} %all_to_all.26), calls=%async_computation.1 | async-start | bytes 6291456 | tf_op jit(solution)/shard_map/all_to_all | solution.py:41
  27.5 0.0 copy-done.2
  27.5 1.3 collective-permute-start.2
  28.8 3.0 collective-permute-start.3
  31.9 0.1 fusion.22
  31.9 0.0 collective-permute-done.2
  31.9 0.7 collective-permute-done.3
  32.7 0.1 fusion.18
  32.8 30.5 %gather_fusion.1 = f32[3072]{0:T(1024)} fusion(f32[3072]{0:T(1024)S(1)} %reshape.142, s32[3072]{0:T(1024)S(1)} %broadcast_clamp_fusion), kind=kCustom, calls=%fused_computation.1 | custom fusion | bytes 36864 | tf_op jit(solution)/shard_map/gather | solution.py:58
  63.3 35.7 %all-to-all-done.1 = f32[8,1,98304]{2,1,0:T(1,128)S(1)} async-done(((f32[8,1,98304]{2,1,0:T(1,128)}), f32[8,1,98304]{2,1,0:T(1,128)S(1)}, u32[]{:S(2)}, u32[]{:S(2)}) %all-to-all-start.1) | async-done | bytes 3145760 | tf_op jit(solution)/shard_map/all_to_all | solution.py:41
  99.0 32.2 %all-to-all-start.3 = ((f32[8,1,384]{2,1,0:T(1,128)}), f32[8,1,384]{2,1,0:T(1,128)S(1)}, u32[]{:S(2)}, u32[]{:S(2)}) async-start(f32[8,1,384]{2,1,0:T(1,128)} %bitcast.16), calls=%async_computation.3 | async-start | bytes 24576 | tf_op jit(solution)/shard_map/all_to_all | solution.py:65
  131.3 10.5 %reduce = f32[8,98304]{1,0:T(8,128)} reduce(f32[8,1,98304]{2,1,0:T(1,128)S(1)} %all-to-all-done.1, f32[]{:T(128)} %constant.31), dimensions={1}, to_apply=%all_to_all.27.reduce_sub_computation | reduce | bytes 6291460 | tf_op jit(solution)/shard_map/all_to_all | solution.py:41
  141.7 4.0 reshape.163
  145.7 14.6 %scatter_custom_fusion = f32[3072,256]{1,0:T(8,128)S(1)} fusion(s32[3072]{0:T(1024)S(1)} %bitcast.43, f32[3072,256]{1,0:T(8,128)} %reshape.163, f32[]{:T(128)} %constant.8.clone.1), kind=kCustom, calls=%fused_computation.12 | custom fusion | bytes 3146240 | tf_op jit(solution)/shard_map/scatter | solution.py:49
  160.3 0.5 broadcast_multiply_fusion
  160.8 0.6 fusion.20
  161.5 1.3 collective-permute-start
  162.8 3.1 collective-permute-start.1
  165.9 0.6 fusion.21
  166.5 0.0 collective-permute-done
  166.5 0.5 collective-permute-done.1
  167.0 1.3 fusion.4
  168.3 12.4 %gather_fusion = f32[3072,256]{1,0:T(8,128)} fusion(f32[3072,256]{1,0:T(8,128)S(1)} %bitcast.37, s32[3072]{0:T(1024)S(1)} %broadcast_clamp_fusion), kind=kCustom, calls=%fused_computation | custom fusion | bytes 6303744 | tf_op jit(solution)/shard_map/gather | solution.py:60
  180.7 7.5 %all_to_all.32 = f32[8,1,98304]{2,1,0:T(1,128)} reshape(f32[3072,256]{1,0:T(8,128)} %gather_fusion) | data formatting | bytes 6291456 | tf_op jit(solution)/shard_map/all_to_all | solution.py:64
  188.1 0.0 all-to-all-done.3
  188.1 9.5 %all-to-all-start.2 = ((f32[8,1,98304]{2,1,0:T(1,128)}), f32[8,1,98304]{2,1,0:T(1,128)S(1)}, u32[]{:S(2)}, u32[]{:S(2)}) async-start(f32[8,1,98304]{2,1,0:T(1,128)} %all_to_all.32), calls=%async_computation.2 | async-start | bytes 6291456 | tf_op jit(solution)/shard_map/all_to_all | solution.py:64
  197.7 0.0 all-reduce.11.cloned.1.call-start
  197.7 5.4 %fusion.7 = f32[256,256]{1,0:T(8,128)} fusion(f32[256,4608]{1,0:T(8,128)} %param.7), kind=kOutput, calls=%fused_computation.15 | convolution fusion | flops 605159424 | bytes 4980736 | tf_op jit(solution)/shard_map/dot_general | solution.py:84
  203.1 15.5 %fusion.9 = f32[3072,256]{1,0:T(8,128)} fusion(bf16[3072,4608]{1,0:T(8,128)(2,1)} %param.5, f32[256,4608]{1,0:T(8,128)} %param.7), kind=kOutput, calls=%fused_computation.17 | convolution fusion | flops 7248936960 | bytes 36175872 | tf_op jit(solution)/shard_map/dot_general | solution.py:90
  218.6 0.0 all-reduce.11.cloned.1.call-update
  218.6 0.3 all-reduce.9.cloned.1.call-start
  218.9 50.3 %all-to-all-done.2 = f32[8,1,98304]{2,1,0:T(1,128)S(1)} async-done(((f32[8,1,98304]{2,1,0:T(1,128)}), f32[8,1,98304]{2,1,0:T(1,128)S(1)}, u32[]{:S(2)}, u32[]{:S(2)}) %all-to-all-start.2) | async-done | bytes 3145760 | tf_op jit(solution)/shard_map/all_to_all | solution.py:64
  269.2 10.7 %multiply_reduce_fusion = f32[8,98304]{1,0:T(8,128)} fusion(f32[8,1,98304]{2,1,0:T(1,128)S(1)} %all-to-all-done.2), kind=kLoop, calls=%fused_computation.11 | loop fusion | flops 786432 | bytes 6291456 | tf_op jit(solution)/shard_map/mul | solution.py:96
  279.9 4.2 mul.85
  284.1 27.9 %all-reduce.11.cloned.1.call-done = (f32[256,256]{1,0:T(8,128)}, f32[3072,256]{1,0:T(8,128)}) async-done(((f32[256,256]{1,0:T(8,128)}, f32[3072,256]{1,0:T(8,128)}), (f32[256,256]{1,0:T(8,128)}, f32[3072,256]{1,0:T(8,128)})) %all-reduce.11.cloned.1.call-update) | async-done | bytes 3407888 | tf_op jit(solution)/shard_map/psum | solution.py:83
  312.0 0.0 copy-done.1
  312.0 5.5 %fusion.1 = f32[3072,256]{1,0:T(8,128)S(1)} fusion(f32[256,256]{1,0:T(8,128)} %get-tuple-element.4, f32[3072,256]{1,0:T(8,128)S(1)} %copy-done.1, f32[3072,256]{1,0:T(8,128)} %get-tuple-element.5, f32[3072,256]{1,0:T(8,128)} %mul.85, f32[3072]{0:T(1024)S(1)} %bitcast.45), kind=kOutput, calls=%fused_computation.6 | convolution fusion | flops 2419851264 | bytes 12857344 | tf_op jit(solution)/shard_map/dot_general | solution.py:93
  317.5 0.0 copy-start
  317.5 16.0 %fusion.13 = f32[256,4608]{1,0:T(8,128)} fusion(bf16[3072,4608]{1,0:T(8,128)(2,1)} %param.5, f32[3072,256]{1,0:T(8,128)S(1)} %fusion.1), kind=kOutput, calls=%fused_computation.21 | convolution fusion | flops 7248543744 | bytes 36175872 | tf_op jit(solution)/shard_map/dot_general | solution.py:99
  333.5 0.0 copy-done
  333.5 1.3 fusion.11
  334.8 0.0 all-reduce.9.cloned.1.call-update
  334.8 111.8 %all-reduce.9.cloned.1.call-done = (f32[256,256]{1,0:T(8,128)}, f32[256,4608]{1,0:T(8,128)}) async-done(((f32[256,256]{1,0:T(8,128)}, f32[256,4608]{1,0:T(8,128)}), (f32[256,256]{1,0:T(8,128)}, f32[256,4608]{1,0:T(8,128)})) %all-reduce.9.cloned.1.call-update) | async-done | bytes 4980752 | tf_op jit(solution)/shard_map/psum | solution.py:101
  446.6 12.1 %convolution_divide_fusion = f32[256,4608]{1,0:T(8,128)} fusion(f32[256,256]{1,0:T(8,128)} %get-tuple-element.2, f32[256,4608]{1,0:T(8,128)} %param.7, f32[256,4608]{1,0:T(8,128)} %get-tuple-element.3), kind=kOutput, calls=%fused_computation.3 | convolution fusion | flops 3626237952 | bytes 14417920 | tf_op jit(solution)/shard_map/dot_general | solution.py:102
  (11 shorter events, 0.1 us)
Async XLA Ops:
  8.5 13.8 %all-to-all-start = ((f32[8,1,384]{2,1,0:T(1,128)}), f32[8,1,384]{2,1,0:T(1,128)S(1)}, u32[]{:S(2)}, u32[]{:S(2)}) async-start(f32[8,1,384]{2,1,0:T(1,128)} %bitcast), calls=%async_computation | async-start | bytes 24576 | tf_op jit(solution)/shard_map/all_to_all | solution.py:42
  22.3 5.2 %copy-start.2 = (s32[12,256]{1,0:T(8,128)S(1)}, s32[12,256]{1,0:T(8,128)}, u32[]{:S(2)}) copy-start(s32[12,256]{1,0:T(8,128)} %param.9) | copy-start | bytes 36868
  22.3 76.8 %all-to-all-start.1 = ((f32[8,1,98304]{2,1,0:T(1,128)}), f32[8,1,98304]{2,1,0:T(1,128)S(1)}, u32[]{:S(2)}, u32[]{:S(2)}) async-start(f32[8,1,98304]{2,1,0:T(1,128)} %all_to_all.26), calls=%async_computation.1 | async-start | bytes 6291456 | tf_op jit(solution)/shard_map/all_to_all | solution.py:41
  27.5 4.4 collective-permute-start.2
  28.8 3.8 collective-permute-start.3
  99.0 89.1 %all-to-all-start.3 = ((f32[8,1,384]{2,1,0:T(1,128)}), f32[8,1,384]{2,1,0:T(1,128)S(1)}, u32[]{:S(2)}, u32[]{:S(2)}) async-start(f32[8,1,384]{2,1,0:T(1,128)} %bitcast.16), calls=%async_computation.3 | async-start | bytes 24576 | tf_op jit(solution)/shard_map/all_to_all | solution.py:65
  161.5 5.0 %collective-permute-start = (f32[256,256]{1,0:T(8,128)S(1)}, f32[256,256]{1,0:T(8,128)S(1)}, u32[]{:S(2)}, u32[]{:S(2)}) collective-permute-start(f32[256,256]{1,0:T(8,128)S(1)} %get-tuple-element.9), channel_id=1, source_target_pairs={{1,0},{2,1},{3,2},{4,3},{5,4},{6,5},{7,6},{9,8},{10,9},{11,10},{12... | collective-permute-start | bytes 786440 | tf_op jit(solution)/shard_map/ppermute | solution.py:13
  162.8 4.2 collective-permute-start.1
  188.1 81.1 %all-to-all-start.2 = ((f32[8,1,98304]{2,1,0:T(1,128)}), f32[8,1,98304]{2,1,0:T(1,128)S(1)}, u32[]{:S(2)}, u32[]{:S(2)}) async-start(f32[8,1,98304]{2,1,0:T(1,128)} %all_to_all.32), calls=%async_computation.2 | async-start | bytes 6291456 | tf_op jit(solution)/shard_map/all_to_all | solution.py:64
  197.7 114.3 %all-reduce.11.cloned.1.call-start = ((), (), s32[]{:S(2)}) async-start(), calls=%async_computation.5 | async-start | bytes 6815744 | tf_op jit(solution)/shard_map/psum | solution.py:83
  218.6 228.0 %all-reduce.9.cloned.1.call-start = ((), (), s32[]{:S(2)}) async-start(), calls=%async_computation.4 | async-start | bytes 9961472 | tf_op jit(solution)/shard_map/psum | solution.py:101
  279.9 32.0 %copy-start.1 = (f32[3072,256]{1,0:T(8,128)S(1)}, f32[3072,256]{1,0:T(8,128)}, u32[]{:S(2)}) copy-start(f32[3072,256]{1,0:T(8,128)} %param.6) | copy-start | bytes 9437188
  317.5 16.0 %copy-start = (f32[3072,256]{1,0:T(8,128)}, f32[3072,256]{1,0:T(8,128)S(1)}, u32[]{:S(2)}) copy-start(f32[3072,256]{1,0:T(8,128)S(1)} %fusion.1) | copy-start | bytes 9437188
Sparse Core Ops, SparseCore 0:
  218.7 93.1 all-reduce.10
  334.9 111.6 all-reduce.8
where the time goes:
time: 475 us; the launch traced here: 466 us
  waiting for transfers between devices  227 us (48%)
  local copies, waits for them, and re-layouts  81.9 us (17%)
  starting transfers between devices  62.3 us (13%)
  matrix products  55.7 us (12%)
  other arithmetic  24.4 us (5%)
  between operations  14.6 us (3%)
    psum x1, waiting for transfers between devices, on_device(): cross, fac_gram = lax.psum((cross_part, gram_part), 'bin')  112 us
    all_to_all x1, waiting for transfers between devices, stencil_term(): lax.all_to_all(back_send, 'bin', split_axis=0, concat_axis=0, tiled=True)  50.3 us
    all_to_all x1, waiting for transfers between devices, stencil_term(): lax.all_to_all(payload, 'bin', split_axis=0, concat_axis=0, tiled=True)  35.7 us
    all_to_all x1, starting transfers between devices, stencil_term(): lax.all_to_all(back_degree.reshape(bin_count, group_size), 'bin', split_a...  32.2 us
    gather x1, local copies, waits for them, and re-layouts, stencil_term(): back_degree = degree_grid.reshape(row_count)[tile_slot]  30.5 us
    psum x1, waiting for transfers between devices, on_device(): lax.psum(lax.dot_general(load_bf, load_bf, right_dims, preferred_element_...  27.9 us
    dot_general x1, matrix products, on_device(): lax.dot_general(fac_bf, counts, left_dims, preferred_element_type=jnp.flo...  16 us
    dot_general x1, matrix products, on_device(): lax.dot_general(counts, load_bf, right_dims, preferred_element_type=jnp.f...  15.5 us
  transfers between devices with their start and end apart: 10, of which 6 were waited for; matrix products, arithmetic and copies ran while one was open for 24% of the time, Pallas kernels for 0%

commit v1 on v0

v1 whole, which is shorter than its diff:
```python
import functools
import jax
import jax.numpy as jnp
from jax import lax
from jax.experimental import pallas as pl
from jax.experimental.pallas import tpu as pltpu
from jax.sharding import PartitionSpec as P

K = 256
G = 18432
PENALTY = float(G * K) / 64.0
EXTRA = 8
CHUNKS = 6
VMEM = 48 * 1024 * 1024
MINOR = (((1,), (1,)), ((), ()))
PLAIN = (((1,), (0,)), ((), ()))
F32 = jnp.float32
BF16 = jnp.bfloat16


def dot(a, b, dims, precision=None):
    return lax.dot_general(a, b, dims, precision=precision, preferred_element_type=F32)


def kernel_call(body, out_shape, flops, nbytes, **kw):
    return pl.pallas_call(
        body,
        out_shape=out_shape,
        compiler_params=pltpu.CompilerParams(vmem_limit_bytes=VMEM),
        cost_estimate=pl.CostEstimate(flops=int(flops), bytes_accessed=int(nbytes), transcendentals=0),
        **kw,
    )


def shape(*dims, dtype=F32):
    return jax.ShapeDtypeStruct(dims, dtype)


SMEM_SPEC = pl.BlockSpec(memory_space=pltpu.SMEM)


def pack(factors, position, me, width, bins):
    rows, width_all = factors.shape
    group = rows // bins
    lanes = 128 if width_all % 128 == 0 and 128 % width == 0 else width_all

    def body(me_ref, fac_ref, pos_ref, out_ref, turned):
        turned[...] = fac_ref[...].T
        first = pl.multiple_of(lax.rem(me_ref[0] * width, lanes), width)
        out_ref[0, :width, :] = turned[pl.ds(first, width), :]
        out_ref[0, width:, :] = jnp.broadcast_to(pos_ref[0], (EXTRA, group))

    grid_spec = pltpu.PrefetchScalarGridSpec(
        num_scalar_prefetch=1,
        grid=(bins,),
        in_specs=[
            pl.BlockSpec((group, lanes), lambda t, m: (t, m[0] * width // lanes)),
            pl.BlockSpec((1, 1, group), lambda t, m: (t, 0, 0)),
        ],
        out_specs=pl.BlockSpec((1, width + EXTRA, group), lambda t, m: (t, 0, 0)),
        scratch_shapes=[pltpu.VMEM((lanes, group), F32)],
    )
    return kernel_call(
        body, shape(bins, width + EXTRA, group), 0, 6 * rows * width * 4, grid_spec=grid_spec
    )(me, factors, position.astype(F32).reshape(bins, 1, group))


def to_grid(got, edge_codes, bin_me):
    bins, wide, group = got.shape
    width = wide - EXTRA
    grid_rows, grid_cols = edge_codes.shape
    rows = bins * group

    def body(me_ref, got_ref, code_ref, grid_ref, first_ref, last_ref, cell_ref, masked):
        block = jnp.concatenate([got_ref[s] for s in range(bins)], axis=1)
        cell = block[width : width + 1].astype(jnp.int32) - me_ref[0] * rows
        cell_ref[...] = cell
        at_row, at_col = cell // grid_cols, cell % grid_cols
        col_hot = jnp.where(
            lax.broadcasted_iota(jnp.int32, (grid_cols, rows), 0) == at_col, 1.0, 0.0
        ).astype(BF16)
        values = block[:width]
        high = values.astype(BF16)
        both = jnp.concatenate([high, (values - high.astype(F32)).astype(BF16)], axis=0)
        for r in range(grid_rows):
            mask = jnp.where(at_row == r, 1.0, 0.0).astype(BF16)
            masked[r * 2 * width : (r + 1) * 2 * width, :] = both * mask
        placed = dot(masked[...], col_hot, MINOR)
        scale = code_ref[...].astype(F32) / 8.0
        for r in range(grid_rows):
            at = r * 2 * width
            line = placed[at : at + width] + placed[at + width : at + 2 * width]
            row_scale = scale[r : r + 1]
            weighted = jnp.concatenate(
                [line * row_scale, jnp.broadcast_to(row_scale, (EXTRA, grid_cols))], axis=0
            )
            grid_ref[r] = weighted
            if r == 0:
                first_ref[...] = weighted
            if r == grid_rows - 1:
                last_ref[...] = weighted

    vm = pl.BlockSpec(memory_space=pltpu.VMEM)
    return kernel_call(
        body,
        (
            shape(grid_rows, wide, grid_cols),
            shape(wide, grid_cols),
            shape(wide, grid_cols),
            shape(1, rows, dtype=jnp.int32),
        ),
        4 * rows * rows * width,
        8 * rows * wide,
        in_specs=[SMEM_SPEC, vm, vm],
        out_specs=(vm, vm, vm, vm),
        scratch_shapes=[pltpu.VMEM((grid_rows * 2 * width, rows), BF16)],
    )(bin_me, got, edge_codes)


def from_grid(grid, above, below, cell, edge_codes, bins):
    grid_rows, wide, grid_cols = grid.shape
    rows = cell.shape[1]
    group = rows // bins

    def body(grid_ref, above_ref, below_ref, cell_ref, code_ref, out_ref, halves):
        scale = code_ref[...].astype(F32) / 8.0
        lane = lax.broadcasted_iota(jnp.int32, (wide, grid_cols), 1)
        for r in range(grid_rows):
            here = grid_ref[r]
            upper = above_ref[...] if r == 0 else grid_ref[r - 1]
            lower = below_ref[...] if r == grid_rows - 1 else grid_ref[r + 1]
            left = jnp.where(lane == 0, 0.0, pltpu.roll(here, 1, 1))
            right = jnp.where(lane == grid_cols - 1, 0.0, pltpu.roll(here, grid_cols - 1, 1))
            value = scale[r : r + 1] * (left + right + 0.5 * (upper + lower))
            high = value.astype(BF16)
            halves[r * wide : (r + 1) * wide, :grid_cols] = high
            halves[r * wide : (r + 1) * wide, grid_cols:] = (value - high.astype(F32)).astype(BF16)
        cell = cell_ref[...]
        at_row, at_col = cell // grid_cols, cell % grid_cols
        for s in range(bins // 2):
            lo, hi = 2 * s * group, (2 * s + 2) * group
            hot = jnp.where(
                lax.broadcasted_iota(jnp.int32, (grid_cols, hi - lo), 0) == at_col[:, lo:hi], 1.0, 0.0
            ).astype(BF16)
            lines = dot(halves[...], jnp.concatenate([hot, hot], axis=0), PLAIN)
            row_here = at_row[:, lo:hi]
            total = jnp.zeros((wide, hi - lo), F32)
            for r in range(grid_rows):
                total = total + jnp.where(row_here == r, lines[r * wide : (r + 1) * wide], 0.0)
            out_ref[2 * s] = total[:, :group]
            out_ref[2 * s + 1] = total[:, group:]

    vm = pl.BlockSpec(memory_space=pltpu.VMEM)
    return kernel_call(
        body,
        shape(bins, wide, group),
        4 * rows * rows * wide,
        8 * rows * wide,
        in_specs=[vm] * 5,
        out_specs=vm,
        scratch_shapes=[pltpu.VMEM((grid_rows * wide, 2 * grid_cols), BF16)],
    )(grid, above, below, cell, edge_codes)


def numer_part(counts, loadings, me, genes_n, half, send_ids, with_gram):
    rows, genes = counts.shape
    width_all = loadings.shape[0]
    width = width_all // genes_n
    step = 256
    steps = rows // 2 // step
    keep_ids = [k for k in range(genes_n) if k not in send_ids]
    total_cols = (steps + with_gram) * step

    def body(me_ref, counts_ref, load_ref, send_ref, keep_ref, load_bf):
        at = pl.program_id(0)

        @pl.when(at == 0)
        def _():
            for k in range(genes_n):
                first = pl.multiple_of((k ^ me_ref[0]) * width, width)
                load_bf[k * width : (k + 1) * width, :] = load_ref[pl.ds(first, width), :].astype(BF16)

        def put(other):
            part = dot(load_bf[...], other, MINOR)
            for i, k in enumerate(send_ids):
                send_ref[i] = part[k * width : (k + 1) * width]
            for i, k in enumerate(keep_ids):
                keep_ref[i] = part[k * width : (k + 1) * width]

        if with_gram:
            pl.when(at < steps)(lambda: put(counts_ref[...]))
            pl.when(at == steps)(lambda: put(load_ref[...].astype(BF16)))
        else:
            put(counts_ref[...])

    out_spec = pl.BlockSpec((genes_n // 2, width, step), lambda i, m: (0, 0, i))
    grid_spec = pltpu.PrefetchScalarGridSpec(
        num_scalar_prefetch=1,
        grid=(steps + with_gram,),
        in_specs=[
            pl.BlockSpec((step, genes), lambda i, m: (jnp.minimum(i, steps - 1) + half * steps, 0)),
            pl.BlockSpec((width_all, genes), lambda i, m: (0, 0)),
        ],
        out_specs=(out_spec, out_spec),
        scratch_shapes=[pltpu.VMEM((width_all, genes), BF16)],
    )
    out = shape(genes_n // 2, width, total_cols)
    return kernel_call(
        body,
        (out, out),
        2 * total_cols * genes * width_all,
        rows * genes + 4 * genes * width_all + 4 * total_cols * width_all,
        grid_spec=grid_spec,
    )(me, counts, loadings)


def swap(block, axis, bit):
    return lax.ppermute(block, axis, [(i, i ^ bit) for i in range(lax.axis_size(axis))])


def scatter_sum(send, keep, send_ids, keep_ids, bits):
    got = swap(send, "gene", bits[0])
    for bit in bits[1:]:
        out_ids = [i for i, k in enumerate(keep_ids) if k & bit]
        in_ids = [i for i, k in enumerate(keep_ids) if not k & bit]
        pick = lambda x, ids: jnp.stack([x[i] for i in ids])
        send = pick(keep, out_ids) + pick(got, out_ids)
        keep = pick(keep, in_ids) + pick(got, in_ids)
        keep_ids = [keep_ids[i] for i in in_ids]
        got = swap(send, "gene", bit)
    return keep[0] + got[0]


def gather_blocks(block, bits):
    have, ids = block[None], [0]
    for bit in bits[:-1]:
        have = jnp.concatenate([have, swap(have, "gene", bit)])
        ids = ids + [k | bit for k in ids]
    return have, ids, swap(have, "gene", bits[-1]), [k | bits[-1] for k in ids]


def new_factors(payload, back, numer, gram, factors, half):
    bins, wide, group = payload.shape
    width = wide - EXTRA
    cols = numer.shape[1]
    steps = bins // 4
    width_all = factors.shape[1]

    def body(pay_ref, back_ref, numer_ref, gram_ref, fac_ref, out_ref):
        plain = dot(gram_ref[...], fac_ref[...], MINOR, lax.Precision.HIGHEST)
        pay = jnp.concatenate([pay_ref[0], pay_ref[1]], axis=1)
        got = jnp.concatenate([back_ref[0], back_ref[1]], axis=1)
        fac, smooth, degree = pay[:width], got[:width], got[width : width + 1]
        out_ref[...] = (
            fac * (numer_ref[...] + PENALTY * smooth) / (plain + PENALTY * degree * fac)
        )

    pair = pl.BlockSpec((2, wide, group), lambda i: (i + half * steps, 0, 0))
    return kernel_call(
        body,
        shape(width, steps * 2 * group),
        12 * width * width_all * steps * 2 * group,
        4 * steps * 2 * group * (width_all + 4 * width),
        grid=(steps,),
        in_specs=[
            pair,
            pair,
            pl.BlockSpec((width, 2 * group), lambda i: (0, i)),
            pl.BlockSpec((width, width_all), lambda i: (0, 0)),
            pl.BlockSpec((2 * group, width_all), lambda i: (i + half * steps, 0)),
        ],
        out_specs=pl.BlockSpec((width, 2 * group), lambda i: (0, i)),
    )(payload, back, numer, gram, factors)


def rounded(parts, ids, width):
    cols = parts[0].shape[2]
    blocks = len(ids[0]) + len(ids[1])

    def body(a0, a1, b0, b1, out_ref):
        for j, (x, y) in enumerate(((a0, a1), (b0, b1))):
            for ref, its in ((x, ids[2 * j]), (y, ids[2 * j + 1])):
                for i, k in enumerate(its):
                    out_ref[k * width : (k + 1) * width, j * cols : (j + 1) * cols] = ref[i].astype(BF16)

    vm = pl.BlockSpec(memory_space=pltpu.VMEM)
    return kernel_call(
        body,
        shape(blocks * width, 2 * cols, dtype=BF16),
        0,
        blocks * width * 2 * cols * 6,
        in_specs=[vm] * 4,
        out_specs=vm,
    )(*parts)


def turned_back(parts, ids, width, me):
    cols = parts[0].shape[2]
    blocks = len(ids[0]) + len(ids[1])
    step = 384
    steps = cols // step

    def body(me_ref, a0, a1, b0, b1, out_ref, block):
        at = pl.program_id(0)

        def put(refs, its):
            for ref, ks in zip(refs, its):
                for i, k in enumerate(ks):
                    first = pl.multiple_of((k ^ me_ref[0]) * width, width)
                    block[pl.ds(first, width), :] = ref[i]

        pl.when(at < steps)(lambda: put((a0, a1), ids[:2]))
        pl.when(at >= steps)(lambda: put((b0, b1), ids[2:]))
        out_ref[...] = block[...].T

    spec_a = pl.BlockSpec((blocks // 2, width, step), lambda i, m: (0, 0, jnp.minimum(i, steps - 1)))
    spec_b = pl.BlockSpec((blocks // 2, width, step), lambda i, m: (0, 0, jnp.maximum(i - steps, 0)))
    grid_spec = pltpu.PrefetchScalarGridSpec(
        num_scalar_prefetch=1,
        grid=(2 * steps,),
        in_specs=[spec_a, spec_a, spec_b, spec_b],
        out_specs=pl.BlockSpec((step, blocks * width), lambda i, m: (i, 0)),
        scratch_shapes=[pltpu.VMEM((blocks * width, step), F32)],
    )
    return kernel_call(
        body,
        shape(2 * cols, blocks * width),
        0,
        blocks * width * 2 * cols * 8,
        grid_spec=grid_spec,
    )(me, *parts)


def cross_part(fac_bf, counts, core, chunk, cols, with_gram):
    width_all, rows = fac_bf.shape
    half = width_all // 2
    extra = width_all if with_gram else 0

    def body(core_ref, fac_ref, counts_ref, send_ref, keep_ref):
        for ref, which in ((send_ref, 1 - core_ref[0]), (keep_ref, core_ref[0])):
            mine = fac_ref[pl.ds(pl.multiple_of(which * half, half), half), :]
            ref[:, :cols] = dot(mine, counts_ref[...], PLAIN)
            if with_gram:
                ref[:, cols:] = dot(mine, fac_ref[...], MINOR)

    out_spec = pl.BlockSpec((half, cols + extra), lambda i, c: (0, 0))
    grid_spec = pltpu.PrefetchScalarGridSpec(
        num_scalar_prefetch=1,
        grid=(1,),
        in_specs=[
            pl.BlockSpec((width_all, rows), lambda i, c: (0, 0)),
            pl.BlockSpec((rows, cols), lambda i, c: (0, chunk)),
        ],
        out_specs=(out_spec, out_spec),
    )
    return kernel_call(
        body,
        (shape(half, cols + extra),) * 2,
        2 * rows * width_all * (cols + extra),
        2 * rows * (cols + width_all) + 4 * width_all * (cols + extra),
        grid_spec=grid_spec,
    )(core, fac_bf, counts)


def bin_sum(send, keep):
    bins = lax.axis_size("bin")
    line = bins // 2
    own = keep + swap(send, "bin", 1)
    total, got = own, None
    for step in range(1, line):
        hops = [(step - 1, step), (line - step, line - step - 1)]
        route = [(2 * a + c, 2 * b + c) for a, b in hops for c in range(2)]
        got = lax.ppermute(own if got is None else own + got, "bin", route)
        total = total + got
    return total, swap(total, "bin", 1)


def new_loadings(loadings, mine, other, gram_mine, gram_other, before, flags, genes_n, chunk, cols):
    width_all, genes = loadings.shape
    width = width_all // genes_n
    half = width_all // 2

    def body(flag_ref, load_ref, mine_ref, other_ref, gm_ref, go_ref, *rest):
        out_ref, load, cross, gram = rest[-4:]
        me, core = flag_ref[0], flag_ref[1]
        at_mine = pl.ds(pl.multiple_of(core * half, half), half)
        at_other = pl.ds(pl.multiple_of((1 - core) * half, half), half)
        cross[at_mine, :] = mine_ref[...]
        cross[at_other, :] = other_ref[...]
        gram[at_mine, :] = gm_ref[...]
        gram[at_other, :] = go_ref[...]
        firsts = [pl.multiple_of((k ^ me) * width, width) for k in range(genes_n)]
        for k, first in enumerate(firsts):
            load[k * width : (k + 1) * width, :] = load_ref[pl.ds(first, width), :]
        below = dot(gram[...], load[...], PLAIN, lax.Precision.HIGHEST)
        cross[...] = load[...] * cross[...] / below
        for k, first in enumerate(firsts):
            out_ref[pl.ds(first, width), :] = cross[k * width : (k + 1) * width, :]

    full = pl.BlockSpec((width_all, cols), lambda i, f: (0, chunk))
    part = pl.BlockSpec((half, cols), lambda i, f: (0, 0))
    gram_at = gram_mine.shape[1] // width_all - 1
    gram_spec = pl.BlockSpec((half, width_all), lambda i, f: (0, gram_at))
    operands = [flags, loadings, mine, other, gram_mine, gram_other]
    in_specs = [full, part, part, gram_spec, gram_spec]
    aliases = {}
    if before is not None:
        operands.append(before)
        in_specs.append(pl.BlockSpec(memory_space=pl.ANY))
        aliases = {len(operands) - 1: 0}
    grid_spec = pltpu.PrefetchScalarGridSpec(
        num_scalar_prefetch=1,
        grid=(1,),
        in_specs=in_specs,
        out_specs=full,
        scratch_shapes=[
            pltpu.VMEM((width_all, cols), F32),
            pltpu.VMEM((width_all, cols), F32),
            pltpu.VMEM((width_all, width_all), F32),
        ],
    )
    return kernel_call(
        body,
        shape(width_all, genes),
        12 * width_all * width_all * cols,
        12 * width_all * cols,
        grid_spec=grid_spec,
        input_output_aliases=aliases,
    )(*operands)


def on_device(counts, factors, loadings, position, edge_codes):
    bins, genes_n = lax.axis_size("bin"), lax.axis_size("gene")
    me, bin_me = lax.axis_index("gene"), lax.axis_index("bin")
    rows, width_all = factors.shape
    genes = counts.shape[1]
    width = width_all // genes_n
    scalar = lambda x: jnp.asarray(x, jnp.int32).reshape(1)
    me1, bin1, core1 = scalar(me), scalar(bin_me), scalar(bin_me % 2)
    flags = jnp.concatenate([me1, core1])
    bits = [1 << b for b in range(genes_n.bit_length() - 1)]
    orders = (bits, bits[::-1])

    payload = pack(factors, position, me1, width, bins)
    got = lax.all_to_all(payload, "bin", split_axis=0, concat_axis=0, tiled=True)

    numer, gram = [], None
    for half in (0, 1):
        bit = orders[half][0]
        send_ids = [k for k in range(genes_n) if k & bit]
        keep_ids = [k for k in range(genes_n) if not k & bit]
        send, keep = numer_part(counts, loadings, me1, genes_n, half, send_ids, half == 0)
        numer.append(scatter_sum(send, keep, send_ids, keep_ids, orders[half]))
    gram = numer[0][:, rows // 2 :]

    grid, first, last, cell = to_grid(got, edge_codes, bin1)
    above = lax.ppermute(last, "bin", [(i, i + 1) for i in range(bins - 1)])
    below = lax.ppermute(first, "bin", [(i + 1, i) for i in range(bins - 1)])
    smooth = from_grid(grid, above, below, cell, edge_codes, bins)
    back = lax.all_to_all(smooth, "bin", split_axis=0, concat_axis=0, tiled=True)

    parts, ids = [], []
    for half in (0, 1):
        block = new_factors(payload, back, numer[half], gram, factors, half)
        have, have_ids, more, more_ids = gather_blocks(block, orders[half][::-1])
        parts += [have, more]
        ids += [have_ids, more_ids]
    fac_bf = rounded(parts, ids, width)
    factors_new = turned_back(parts, ids, width, me1)

    cols = genes // CHUNKS
    loadings_new = None
    for chunk in range(CHUNKS):
        send, keep = cross_part(fac_bf, counts, core1, chunk, cols, chunk == 0)
        mine, other = bin_sum(send, keep)
        if chunk == 0:
            gram_mine, gram_other = mine, other
            gram_mine, gram_other = mine[:, cols:], other[:, cols:]
        loadings_new = new_loadings(
            loadings, mine, other, gram_mine, gram_other, loadings_new, flags, genes_n, chunk, cols
        )
    return factors_new, loadings_new


def solution(mesh):
    placed = (P("bin", "gene"), P("bin", None), P(None, "gene"), P("bin"), P("bin", None))
    return jax.shard_map(
        on_device,
        mesh=mesh,
        in_specs=placed,
        out_specs=(P("bin", None), P(None, "gene")),
        check_vma=False,
    )
```

time: 475 us -> 284 us (0.60); the launches traced: 466 us -> 283 us
  waiting for transfers between devices: 227 us -> 138 us
  Pallas kernels: 0 us -> 80 us
  local copies, waits for them, and re-layouts: 81.9 us -> 6.88 us
  matrix products: 55.7 us -> 0 us
  other arithmetic: 24.4 us -> 7.09 us
  between operations: 14.6 us -> 1.24 us
  starting transfers between devices: 62.3 us -> 49.5 us
    psum x2 -> x0, waiting for transfers between devices: 140 us -> none  [the longest x1 112 us: on_device(): cross, fac_gram = lax.psum((cross_part, gram_part), 'bin')]
    ppermute x4 -> x40, waiting for transfers between devices: 1.22 us -> 134 us  [the longest x18 90.7 us: bin_sum(): got = lax.ppermute(own if got is None else own + got, 'bin', route)]
    all_to_all x4 -> x2, waiting for transfers between devices: 86.1 us -> 4.59 us  [the longest x1 4.59 us: on_device(): lax.all_to_all(smooth, 'bin', split_axis=0, concat_axis=0, tiled=True)]
    pallas_call x0 -> x21, Pallas kernels: none -> 80 us  [the longest x6 23.4 us: cross_part(): kernel_call(body, (shape(half, cols + extra),) * 2, 2 * rows * width_all...]
    dot_general x6 -> x0, matrix products: 55.7 us -> none  [the longest x1 16 us: on_device(): lax.dot_general(fac_bf, counts, left_dims, preferred_element_type=jnp.flo...]
    gather x2 -> x0, local copies, waits for them, and re-layouts: 42.9 us -> none  [the longest x1 30.5 us: stencil_term(): back_degree = degree_grid.reshape(row_count)[tile_slot]]
    all_to_all x4 -> x2, starting transfers between devices: 53.3 us -> 13.2 us  [the longest x1 6.92 us: on_device(): lax.all_to_all(smooth, 'bin', split_axis=0, concat_axis=0, tiled=True)]
    ppermute x4 -> x40, starting transfers between devices: 8.67 us -> 36.3 us  [the longest x18 23 us: bin_sum(): got = lax.ppermute(own if got is None else own + got, 'bin', route)]
  transfers between devices with their start and end apart: 10 -> 42, of which waited for: 6 -> 18; matrix products, arithmetic and copies ran while one was open for 24% -> 2% of each run, Pallas kernels for 0% -> 23%
where the time goes in v1:
time: 284 us; the launch traced here: 283 us
  waiting for transfers between devices  138 us (49%)
  Pallas kernels  80 us (28%)
  starting transfers between devices  49.5 us (17%)
  other arithmetic  7.09 us (2%)
  local copies, waits for them, and re-layouts  6.88 us (2%)
    ppermute x18, waiting for transfers between devices, bin_sum(): got = lax.ppermute(own if got is None else own + got, 'bin', route)  90.7 us
    ppermute x20, waiting for transfers between devices, swap(): lax.ppermute(block, axis, [(i, i ^ bit) for i in range(lax.axis_size(axis...  39.5 us
    pallas_call x6, Pallas kernels, cross_part(): kernel_call(body, (shape(half, cols + extra),) * 2, 2 * rows * width_all...  23.4 us
    ppermute x18, starting transfers between devices, bin_sum(): got = lax.ppermute(own if got is None else own + got, 'bin', route)  23 us
    pallas_call x2, Pallas kernels, numer_part(): kernel_call(body, (out, out), 2 * total_cols * genes * width_all, rows *...  22.9 us
    pallas_call x6, Pallas kernels, new_loadings(): kernel_call(body, shape(width_all, genes), 12 * width_all * width_all * c...  14.3 us
    ppermute x20, starting transfers between devices, swap(): lax.ppermute(block, axis, [(i, i ^ bit) for i in range(lax.axis_size(axis...  10.1 us
    all_to_all x1, starting transfers between devices, on_device(): lax.all_to_all(smooth, 'bin', split_axis=0, concat_axis=0, tiled=True)  6.92 us
  transfers between devices with their start and end apart: 42, of which 18 were waited for; matrix products, arithmetic and copies ran while one was open for 2% of the time, Pallas kernels for 23%

profile of v1, /device:TPU:0, one launch (start us, length us, event | category | flops | bytes accessed | tf_op | source)
XLA Modules:
  0.0 283.0 jit_solution(38461282974113400)
XLA Ops:
  1.3 1.9 copy-done
  3.2 3.4 %shard_map.68.pay_ref = f32[8,72,384]{2,1,0:T(8,128)} custom-call(s32[1]{0:T(128)} %bitcast.me_ref, f32[3072,256]{1,0:T(8,128)S(1)} %copy-done, f32[8,1,384]{2,1,0:T(1,128)S(1)} %bitcast.16), custom_call_target="tpu_custom_call" | custom-call | bytes 4718592 | tf_op jit(solution)/shard_map/pallas_call | solution.py:63
  6.6 6.3 %all-to-all-start = ((f32[8,72,384]{2,1,0:T(8,128)}), f32[8,72,384]{2,1,0:T(8,128)S(1)}, u32[]{:S(2)}, u32[]{:S(2)}) async-start(f32[8,72,384]{2,1,0:T(8,128)} %shard_map.68.pay_ref), calls=%async_computation | async-start | bytes 1769472 | tf_op jit(solution)/shard_map/all_to_all | solution.py:445
  13.0 11.1 %shard_map.73 = (f32[2,64,1536]{2,1,0:T(8,128)}, f32[2,64,1536]{2,1,0:T(8,128)S(1)}) custom-call(s32[1]{0:T(128)} %bitcast.me_ref, bf16[3072,4608]{1,0:T(8,128)(2,1)} %counts_ref.15, f32[256,4608]{1,0:T(8,128)} %load_ref.15), custom_call_target="tpu_custom_call" | custom-call | flops 3623878656 | bytes 20447232 | tf_op jit(solution)/shard_map/pallas_call | solution.py:208
  24.9 1.5 collective-permute-start.6
  26.4 11.9 %shard_map.71 = (f32[2,64,1792]{2,1,0:T(8,128)}, f32[2,64,1792]{2,1,0:T(8,128)S(1)}) custom-call(s32[1]{0:T(128)} %bitcast.me_ref, bf16[3072,4608]{1,0:T(8,128)(2,1)} %counts_ref.15, f32[256,4608]{1,0:T(8,128)} %load_ref.15), custom_call_target="tpu_custom_call" | custom-call | flops 4227858432 | bytes 20709376 | tf_op jit(solution)/shard_map/pallas_call | solution.py:208
  39.2 1.5 collective-permute-start.2
  40.7 2.6 shard_map.69
  43.4 1.8 collective-permute-start
  46.5 3.5 %collective-permute-done.1.below_ref = f32[72,256]{1,0:T(8,128)S(1)} collective-permute-done((f32[72,256]{1,0:T(8,128)S(1)}, f32[72,256]{1,0:T(8,128)S(1)}, u32[]{:S(2)}, u32[]{:S(2)}) %collective-permute-start.1) | collective-permute-done | bytes 73760 | tf_op jit(solution)/shard_map/ppermute | solution.py:458
  50.1 3.2 %shard_map.70 = f32[8,72,384]{2,1,0:T(8,128)S(1)} custom-call(f32[12,72,256]{2,1,0:T(8,128)S(1)} %get-tuple-element.22.grid_ref, f32[72,256]{1,0:T(8,128)S(1)} %collective-permute-done.above_ref, f32[72,256]{1,0:T(8,128)S(1)} %collective-permute-done.1.below_ref, s32[1,3072]{1,0:T(1,128)S(1)} %get-tuple-element.25.cell_ref, s32[12,256]{1,0:T(8,128)S(1)} %copy-done.9), custom_call_target="tpu_custom_call" | custom-call | flops 2717908992 | bytes 1769472 | tf_op jit(solution)/shard_map/pallas_call | solution.py:154
  54.2 6.9 %all-to-all-start.1 = ((f32[8,72,384]{2,1,0:T(8,128)}), f32[8,72,384]{2,1,0:T(8,128)}, u32[]{:S(2)}, u32[]{:S(2)}) async-start(f32[8,72,384]{2,1,0:T(8,128)} %copy-done.5), calls=%async_computation.1 | async-start | bytes 1769472 | tf_op jit(solution)/shard_map/all_to_all | solution.py:460
  64.7 9.5 %collective-permute-done.7 = f32[1,64,1536]{2,1,0:T(8,128)S(1)} collective-permute-done((f32[1,64,1536]{2,1,0:T(8,128)S(1)}, f32[1,64,1536]{2,1,0:T(8,128)S(1)}, u32[]{:S(2)}, u32[]{:S(2)}) %collective-permute-start.7) | collective-permute-done | bytes 393248 | tf_op jit(solution)/shard_map/ppermute | solution.py:218
  75.4 2.1 collective-permute-done.3
  80.1 4.6 %all-to-all-done.1.back_ref = f32[8,72,384]{2,1,0:T(8,128)} async-done(((f32[8,72,384]{2,1,0:T(8,128)}), f32[8,72,384]{2,1,0:T(8,128)}, u32[]{:S(2)}, u32[]{:S(2)}) %all-to-all-start.1) | async-done | bytes 884768 | tf_op jit(solution)/shard_map/all_to_all | solution.py:460
  85.6 2.9 %shard_map.74 = f32[64,1536]{1,0:T(8,128)S(1)} custom-call(f32[8,72,384]{2,1,0:T(8,128)} %shard_map.68.pay_ref, f32[8,72,384]{2,1,0:T(8,128)} %all-to-all-done.1.back_ref, f32[64,1536]{1,0:T(8,128)S(1)} %fusion.3.numer_ref, f32[64,256]{1,0:T(8,128)S(1)} %copy-done.7, f32[3072,256]{1,0:T(8,128)S(1)} %copy-done.1), custom_call_target="tpu_custom_call" | custom-call | flops 301989888 | bytes 3145728 | tf_op jit(solution)/shard_map/pallas_call | solution.py:259
  89.1 2.8 shard_map.72
  92.4 7.0 %collective-permute-done.8 = f32[1,64,1536]{2,1,0:T(8,128)S(1)} collective-permute-done((f32[1,64,1536]{2,1,0:T(8,128)S(1)}, f32[1,64,1536]{2,1,0:T(8,128)S(1)}, u32[]{:S(2)}, u32[]{:S(2)}) %collective-permute-start.8) | collective-permute-done | bytes 393248 | tf_op jit(solution)/shard_map/ppermute | solution.py:218
  100.1 3.9 %collective-permute-done.4 = f32[1,64,1536]{2,1,0:T(8,128)S(1)} collective-permute-done((f32[1,64,1536]{2,1,0:T(8,128)S(1)}, f32[1,64,1536]{2,1,0:T(8,128)S(1)}, u32[]{:S(2)}, u32[]{:S(2)}) %collective-permute-start.4) | collective-permute-done | bytes 393248 | tf_op jit(solution)/shard_map/ppermute | solution.py:218
  104.0 1.5 collective-permute-start.5
  105.6 13.9 %collective-permute-done.9.b1 = f32[2,64,1536]{2,1,0:T(8,128)S(1)} collective-permute-done((f32[2,64,1536]{2,1,0:T(8,128)S(1)}, f32[2,64,1536]{2,1,0:T(8,128)S(1)}, u32[]{:S(2)}, u32[]{:S(2)}) %collective-permute-start.9) | collective-permute-done | bytes 786464 | tf_op jit(solution)/shard_map/ppermute | solution.py:218
  119.5 1.5 collective-permute-done.5.a1
  121.1 4.7 %shard_map.78 = (f32[128,1024]{1,0:T(8,128)S(1)}, f32[128,1024]{1,0:T(8,128)S(1)}) custom-call(s32[1]{0:T(128)} %bitcast.7.core_ref, bf16[256,3072]{1,0:T(8,128)(2,1)S(1)} %shard_map.76.fac_ref, bf16[3072,4608]{1,0:T(8,128)(2,1)} %counts_ref.15), custom_call_target="tpu_custom_call" | custom-call | flops 1610612736 | bytes 7340032 | tf_op jit(solution)/shard_map/pallas_call | solution.py:356
  125.8 3.8 %shard_map.82 = (f32[128,768]{1,0:T(8,128)S(1)}, f32[128,768]{1,0:T(8,128)S(1)}) custom-call(s32[1]{0:T(128)} %bitcast.7.core_ref, bf16[256,3072]{1,0:T(8,128)(2,1)S(1)} %shard_map.76.fac_ref, bf16[3072,4608]{1,0:T(8,128)(2,1)} %counts_ref.15), custom_call_target="tpu_custom_call" | custom-call | flops 1207959552 | bytes 7077888 | tf_op jit(solution)/shard_map/pallas_call | solution.py:356
  130.2 3.7 %shard_map.81 = (f32[128,768]{1,0:T(8,128)S(1)}, f32[128,768]{1,0:T(8,128)S(1)}) custom-call(s32[1]{0:T(128)} %bitcast.7.core_ref, bf16[256,3072]{1,0:T(8,128)(2,1)S(1)} %shard_map.76.fac_ref, bf16[3072,4608]{1,0:T(8,128)(2,1)} %counts_ref.15), custom_call_target="tpu_custom_call" | custom-call | flops 1207959552 | bytes 7077888 | tf_op jit(solution)/shard_map/pallas_call | solution.py:356
  134.0 3.7 %shard_map.80 = (f32[128,768]{1,0:T(8,128)S(1)}, f32[128,768]{1,0:T(8,128)S(1)}) custom-call(s32[1]{0:T(128)} %bitcast.7.core_ref, bf16[256,3072]{1,0:T(8,128)(2,1)S(1)} %shard_map.76.fac_ref, bf16[3072,4608]{1,0:T(8,128)(2,1)} %counts_ref.15), custom_call_target="tpu_custom_call" | custom-call | flops 1207959552 | bytes 7077888 | tf_op jit(solution)/shard_map/pallas_call | solution.py:356
  138.3 3.7 %shard_map.79 = (f32[128,768]{1,0:T(8,128)S(1)}, f32[128,768]{1,0:T(8,128)S(1)}) custom-call(s32[1]{0:T(128)} %bitcast.7.core_ref, bf16[256,3072]{1,0:T(8,128)(2,1)S(1)} %shard_map.76.fac_ref, bf16[3072,4608]{1,0:T(8,128)(2,1)} %counts_ref.15), custom_call_target="tpu_custom_call" | custom-call | flops 1207959552 | bytes 7077888 | tf_op jit(solution)/shard_map/pallas_call | solution.py:356
  142.2 1.3 collective-permute-start.16
  143.5 3.7 %shard_map.77 = (f32[128,768]{1,0:T(8,128)S(1)}, f32[128,768]{1,0:T(8,128)S(1)}) custom-call(s32[1]{0:T(128)} %bitcast.7.core_ref, bf16[256,3072]{1,0:T(8,128)(2,1)S(1)} %shard_map.76.fac_ref, bf16[3072,4608]{1,0:T(8,128)(2,1)} %counts_ref.15), custom_call_target="tpu_custom_call" | custom-call | flops 1207959552 | bytes 7077888 | tf_op jit(solution)/shard_map/pallas_call | solution.py:356
  150.7 1.5 collective-permute-start.26
  153.7 10.6 %collective-permute-done.36 = f32[128,768]{1,0:T(8,128)S(1)} collective-permute-done((f32[128,768]{1,0:T(8,128)S(1)}, f32[128,768]{1,0:T(8,128)S(1)}, u32[]{:S(2)}, u32[]{:S(2)}) %collective-permute-start.36) | collective-permute-done | bytes 393248 | tf_op jit(solution)/shard_map/ppermute | solution.py:373
  164.2 4.4 %collective-permute-start.11 = (f32[128,768]{1,0:T(8,128)S(1)}, f32[128,768]{1,0:T(8,128)S(1)}, u32[]{:S(2)}, u32[]{:S(2)}) collective-permute-start(f32[128,768]{1,0:T(8,128)S(1)} %add.131), channel_id=1, source_target_pairs={{0,2},{1,3},{6,4},{7,5},{8,10},{9,11},{14,12},{15,13},{16,18},{17,... | collective-permute-start | bytes 1179656 | tf_op jit(solution)/shard_map/ppermute | solution.py:373
  168.7 4.0 %collective-permute-done.31 = f32[128,768]{1,0:T(8,128)S(1)} collective-permute-done((f32[128,768]{1,0:T(8,128)S(1)}, f32[128,768]{1,0:T(8,128)S(1)}, u32[]{:S(2)}, u32[]{:S(2)}) %collective-permute-start.31) | collective-permute-done | bytes 393248 | tf_op jit(solution)/shard_map/ppermute | solution.py:373
  174.2 6.9 %collective-permute-done.26 = f32[128,768]{1,0:T(8,128)S(1)} collective-permute-done((f32[128,768]{1,0:T(8,128)S(1)}, f32[128,768]{1,0:T(8,128)S(1)}, u32[]{:S(2)}, u32[]{:S(2)}) %collective-permute-start.26) | collective-permute-done | bytes 393248 | tf_op jit(solution)/shard_map/ppermute | solution.py:373
  181.8 7.7 %collective-permute-done.21 = f32[128,768]{1,0:T(8,128)S(1)} collective-permute-done((f32[128,768]{1,0:T(8,128)S(1)}, f32[128,768]{1,0:T(8,128)S(1)}, u32[]{:S(2)}, u32[]{:S(2)}) %collective-permute-start.21) | collective-permute-done | bytes 393248 | tf_op jit(solution)/shard_map/ppermute | solution.py:373
  190.2 7.5 %collective-permute-done.11 = f32[128,768]{1,0:T(8,128)S(1)} collective-permute-done((f32[128,768]{1,0:T(8,128)S(1)}, f32[128,768]{1,0:T(8,128)S(1)}, u32[]{:S(2)}, u32[]{:S(2)}) %collective-permute-start.11) | collective-permute-done | bytes 393248 | tf_op jit(solution)/shard_map/ppermute | solution.py:373
  206.1 10.0 %collective-permute-done.38 = f32[128,768]{1,0:T(8,128)S(1)} collective-permute-done((f32[128,768]{1,0:T(8,128)S(1)}, f32[128,768]{1,0:T(8,128)S(1)}, u32[]{:S(2)}, u32[]{:S(2)}) %collective-permute-start.38) | collective-permute-done | bytes 393248 | tf_op jit(solution)/shard_map/ppermute | solution.py:373
  217.5 7.7 %collective-permute-done.33 = f32[128,768]{1,0:T(8,128)S(1)} collective-permute-done((f32[128,768]{1,0:T(8,128)S(1)}, f32[128,768]{1,0:T(8,128)S(1)}, u32[]{:S(2)}, u32[]{:S(2)}) %collective-permute-start.33) | collective-permute-done | bytes 393248 | tf_op jit(solution)/shard_map/ppermute | solution.py:373
  225.3 8.3 %collective-permute-done.28 = f32[128,768]{1,0:T(8,128)S(1)} collective-permute-done((f32[128,768]{1,0:T(8,128)S(1)}, f32[128,768]{1,0:T(8,128)S(1)}, u32[]{:S(2)}, u32[]{:S(2)}) %collective-permute-start.28) | collective-permute-done | bytes 393248 | tf_op jit(solution)/shard_map/ppermute | solution.py:373
  233.7 28.0 %collective-permute-done.18 = f32[128,1024]{1,0:T(8,128)S(1)} collective-permute-done((f32[128,1024]{1,0:T(8,128)S(1)}, f32[128,1024]{1,0:T(8,128)S(1)}, u32[]{:S(2)}, u32[]{:S(2)}) %collective-permute-start.18) | collective-permute-done | bytes 524320 | tf_op jit(solution)/shard_map/ppermute | solution.py:373
  262.7 1.6 collective-permute-done.19.other_ref
  264.4 4.2 %shard_map.75 = f32[3072,256]{1,0:T(8,128)} custom-call(s32[1]{0:T(128)} %bitcast.me_ref, f32[2,64,1536]{2,1,0:T(8,128)S(1)} %pad_maximum_fusion.a0, f32[2,64,1536]{2,1,0:T(8,128)S(1)} %collective-permute-done.5.a1, f32[2,64,1536]{2,1,0:T(8,128)S(1)} %pad_maximum_fusion.1.b0, f32[2,64,1536]{2,1,0:T(8,128)S(1)} %collective-permute-done.9.b1), custom_call_target="tpu_custom_call" | custom-call | bytes 6291456 | tf_op jit(solution)/shard_map/pallas_call | solution.py:325
  268.7 2.4 shard_map.83.rest_0_
  271.1 2.4 shard_map.84.rest_0_
  273.5 2.4 shard_map.85.rest_0_
  275.9 2.4 shard_map.86.rest_0_
  278.3 2.4 shard_map.87.rest_0_
  280.6 2.4 shard_map.88
  (117 shorter events, 34.9 us)
Async XLA Ops:
  6.6 34.1 %all-to-all-start = ((f32[8,72,384]{2,1,0:T(8,128)}), f32[8,72,384]{2,1,0:T(8,128)S(1)}, u32[]{:S(2)}, u32[]{:S(2)}) async-start(f32[8,72,384]{2,1,0:T(8,128)} %shard_map.68.pay_ref), calls=%async_computation | async-start | bytes 1769472 | tf_op jit(solution)/shard_map/all_to_all | solution.py:445
  24.9 15.8 %copy-start.9 = (s32[12,256]{1,0:T(8,128)S(1)}, s32[12,256]{1,0:T(8,128)}, u32[]{:S(2)}) copy-start(s32[12,256]{1,0:T(8,128)} %code_ref.3) | copy-start | bytes 36868
  24.9 36.3 %collective-permute-start.6 = (f32[2,64,1536]{2,1,0:T(8,128)}, f32[2,64,1536]{2,1,0:T(8,128)}, u32[]{:S(2)}, u32[]{:S(2)}) collective-permute-start(f32[2,64,1536]{2,1,0:T(8,128)} %get-tuple-element.29), channel_id=1, source_target_pairs={{0,16},{8,24},{16,0},{24,8},{1,17},{9,25},{17,1},{25,9},{2,18},{10... | collective-permute-start | bytes 2359304 | tf_op jit(solution)/shard_map/ppermute | solution.py:218
  39.2 23.7 %collective-permute-start.2 = (f32[2,64,1792]{2,1,0:T(8,128)}, f32[2,64,1792]{2,1,0:T(8,128)}, u32[]{:S(2)}, u32[]{:S(2)}) collective-permute-start(f32[2,64,1792]{2,1,0:T(8,128)} %get-tuple-element.27), channel_id=1, source_target_pairs={{0,8},{8,0},{16,24},{24,16},{1,9},{9,1},{17,25},{25,17},{2,10},{10... | collective-permute-start | bytes 2752520 | tf_op jit(solution)/shard_map/ppermute | solution.py:218
  43.4 3.2 %collective-permute-start = (f32[72,256]{1,0:T(8,128)S(1)}, f32[72,256]{1,0:T(8,128)S(1)}, u32[]{:S(2)}, u32[]{:S(2)}) collective-permute-start(f32[72,256]{1,0:T(8,128)S(1)} %get-tuple-element.23), channel_id=1, source_target_pairs={{0,1},{1,2},{2,3},{3,4},{4,5},{5,6},{6,7},{8,9},{9,10},{10,11},{11... | collective-permute-start | bytes 221192 | tf_op jit(solution)/shard_map/ppermute | solution.py:457
  45.2 4.9 %collective-permute-start.1 = (f32[72,256]{1,0:T(8,128)S(1)}, f32[72,256]{1,0:T(8,128)S(1)}, u32[]{:S(2)}, u32[]{:S(2)}) collective-permute-start(f32[72,256]{1,0:T(8,128)S(1)} %get-tuple-element.24), channel_id=1, source_target_pairs={{1,0},{2,1},{3,2},{4,3},{5,4},{6,5},{7,6},{9,8},{10,9},{11,10},{12... | collective-permute-start | bytes 221192 | tf_op jit(solution)/shard_map/ppermute | solution.py:458
  54.2 30.5 %copy-start.1 = (f32[3072,256]{1,0:T(8,128)S(1)}, f32[3072,256]{1,0:T(8,128)}, u32[]{:S(2)}) copy-start(f32[3072,256]{1,0:T(8,128)} %fac_ref.5) | copy-start | bytes 9437188
  54.2 30.5 %all-to-all-start.1 = ((f32[8,72,384]{2,1,0:T(8,128)}), f32[8,72,384]{2,1,0:T(8,128)}, u32[]{:S(2)}, u32[]{:S(2)}) async-start(f32[8,72,384]{2,1,0:T(8,128)} %copy-done.5), calls=%async_computation.1 | async-start | bytes 1769472 | tf_op jit(solution)/shard_map/all_to_all | solution.py:460
  62.3 11.9 %collective-permute-start.7 = (f32[1,64,1536]{2,1,0:T(8,128)S(1)}, f32[1,64,1536]{2,1,0:T(8,128)S(1)}, u32[]{:S(2)}, u32[]{:S(2)}) collective-permute-start(f32[1,64,1536]{2,1,0:T(8,128)S(1)} %slice_add_fusion.2), channel_id=1, source_target_pairs={{0,8},{8,0},{16,24},{24,16},{1,9},{9,1},{17,25},{25,17},{2,10},{10... | collective-permute-start | bytes 1179656 | tf_op jit(solution)/shard_map/ppermute | solution.py:218
  64.2 13.3 %collective-permute-start.3 = (f32[1,64,1792]{2,1,0:T(8,128)S(1)}, f32[1,64,1792]{2,1,0:T(8,128)S(1)}, u32[]{:S(2)}, u32[]{:S(2)}) collective-permute-start(f32[1,64,1792]{2,1,0:T(8,128)S(1)} %slice_add_fusion), channel_id=1, source_target_pairs={{0,16},{8,24},{16,0},{24,8},{1,17},{9,25},{17,1},{25,9},{2,18},{10... | collective-permute-start | bytes 1376264 | tf_op jit(solution)/shard_map/ppermute | solution.py:218
  85.6 3.5 %copy-start.3 = (f32[64,1792]{1,0:T(8,128)S(1)}, f32[64,1792]{1,0:T(8,128)}, u32[]{:S(2)}) copy-start(f32[64,1792]{1,0:T(8,128)} %copy-done.2) | copy-start | bytes 1376260
  85.6 3.5 %copy-start.8 = (f32[64,256]{1,0:T(8,128)S(1)}, f32[64,256]{1,0:T(8,128)}, u32[]{:S(2)}) copy-start(f32[64,256]{1,0:T(8,128)} %slice.46.gram_ref) | copy-start | bytes 196612
  88.4 11.0 %collective-permute-start.8 = (f32[1,64,1536]{2,1,0:T(8,128)S(1)}, f32[1,64,1536]{2,1,0:T(8,128)S(1)}, u32[]{:S(2)}, u32[]{:S(2)}) collective-permute-start(f32[1,64,1536]{2,1,0:T(8,128)S(1)} %bitcast.14), channel_id=1, source_target_pairs={{0,8},{8,0},{16,24},{24,16},{1,9},{9,1},{17,25},{25,17},{2,10},{10... | collective-permute-start | bytes 1179656 | tf_op jit(solution)/shard_map/ppermute | solution.py:218
  91.9 12.1 %collective-permute-start.4 = (f32[1,64,1536]{2,1,0:T(8,128)S(1)}, f32[1,64,1536]{2,1,0:T(8,128)S(1)}, u32[]{:S(2)}, u32[]{:S(2)}) collective-permute-start(f32[1,64,1536]{2,1,0:T(8,128)S(1)} %bitcast.12), channel_id=1, source_target_pairs={{0,16},{8,24},{16,0},{24,8},{1,17},{9,25},{17,1},{25,9},{2,18},{10... | collective-permute-start | bytes 1179656 | tf_op jit(solution)/shard_map/ppermute | solution.py:218
  99.5 20.0 %collective-permute-start.9 = (f32[2,64,1536]{2,1,0:T(8,128)S(1)}, f32[2,64,1536]{2,1,0:T(8,128)S(1)}, u32[]{:S(2)}, u32[]{:S(2)}) collective-permute-start(f32[2,64,1536]{2,1,0:T(8,128)S(1)} %pad_maximum_fusion.1.b0), channel_id=1, source_target_pairs={{0,16},{8,24},{16,0},{24,8},{1,17},{9,25},{17,1},{25,9},{2,18},{10... | collective-permute-start | bytes 2359304 | tf_op jit(solution)/shard_map/ppermute | solution.py:218
  104.0 16.9 %collective-permute-start.5 = (f32[2,64,1536]{2,1,0:T(8,128)S(1)}, f32[2,64,1536]{2,1,0:T(8,128)S(1)}, u32[]{:S(2)}, u32[]{:S(2)}) collective-permute-start(f32[2,64,1536]{2,1,0:T(8,128)S(1)} %pad_maximum_fusion.a0), channel_id=1, source_target_pairs={{0,8},{8,0},{16,24},{24,16},{1,9},{9,1},{17,25},{25,17},{2,10},{10... | collective-permute-start | bytes 2359304 | tf_op jit(solution)/shard_map/ppermute | solution.py:218
  125.8 16.4 %collective-permute-start.15 = (f32[128,1024]{1,0:T(8,128)S(1)}, f32[128,1024]{1,0:T(8,128)S(1)}, u32[]{:S(2)}, u32[]{:S(2)}) collective-permute-start(f32[128,1024]{1,0:T(8,128)S(1)} %get-tuple-element.33), channel_id=1, source_target_pairs={{0,1},{1,0},{2,3},{3,2},{4,5},{5,4},{6,7},{7,6},{8,9},{9,8},{10,11... | collective-permute-start | bytes 1572872 | tf_op jit(solution)/shard_map/ppermute | solution.py:218
  129.7 17.6 %collective-permute-start.35 = (f32[128,768]{1,0:T(8,128)S(1)}, f32[128,768]{1,0:T(8,128)S(1)}, u32[]{:S(2)}, u32[]{:S(2)}) collective-permute-start(f32[128,768]{1,0:T(8,128)S(1)} %get-tuple-element.41), channel_id=1, source_target_pairs={{0,1},{1,0},{2,3},{3,2},{4,5},{5,4},{6,7},{7,6},{8,9},{9,8},{10,11... | collective-permute-start | bytes 1179656 | tf_op jit(solution)/shard_map/ppermute | solution.py:218
  133.9 13.9 %collective-permute-start.30 = (f32[128,768]{1,0:T(8,128)S(1)}, f32[128,768]{1,0:T(8,128)S(1)}, u32[]{:S(2)}, u32[]{:S(2)}) collective-permute-start(f32[128,768]{1,0:T(8,128)S(1)} %get-tuple-element.39), channel_id=1, source_target_pairs={{0,1},{1,0},{2,3},{3,2},{4,5},{5,4},{6,7},{7,6},{8,9},{9,8},{10,11... | collective-permute-start | bytes 1179656 | tf_op jit(solution)/shard_map/ppermute | solution.py:218
  137.8 11.5 %collective-permute-start.25 = (f32[128,768]{1,0:T(8,128)S(1)}, f32[128,768]{1,0:T(8,128)S(1)}, u32[]{:S(2)}, u32[]{:S(2)}) collective-permute-start(f32[128,768]{1,0:T(8,128)S(1)} %get-tuple-element.37), channel_id=1, source_target_pairs={{0,1},{1,0},{2,3},{3,2},{4,5},{5,4},{6,7},{7,6},{8,9},{9,8},{10,11... | collective-permute-start | bytes 1179656 | tf_op jit(solution)/shard_map/ppermute | solution.py:218
  142.0 8.6 %collective-permute-start.20 = (f32[128,768]{1,0:T(8,128)S(1)}, f32[128,768]{1,0:T(8,128)S(1)}, u32[]{:S(2)}, u32[]{:S(2)}) collective-permute-start(f32[128,768]{1,0:T(8,128)S(1)} %get-tuple-element.35), channel_id=1, source_target_pairs={{0,1},{1,0},{2,3},{3,2},{4,5},{5,4},{6,7},{7,6},{8,9},{9,8},{10,11... | collective-permute-start | bytes 1179656 | tf_op jit(solution)/shard_map/ppermute | solution.py:218
  142.2 31.2 %collective-permute-start.16 = (f32[128,1024]{1,0:T(8,128)S(1)}, f32[128,1024]{1,0:T(8,128)S(1)}, u32[]{:S(2)}, u32[]{:S(2)}) collective-permute-start(f32[128,1024]{1,0:T(8,128)S(1)} %add.136), channel_id=1, source_target_pairs={{0,2},{1,3},{6,4},{7,5},{8,10},{9,11},{14,12},{15,13},{16,18},{17,... | collective-permute-start | bytes 1572872 | tf_op jit(solution)/shard_map/ppermute | solution.py:373
  147.3 5.0 %collective-permute-start.10 = (f32[128,768]{1,0:T(8,128)S(1)}, f32[128,768]{1,0:T(8,128)S(1)}, u32[]{:S(2)}, u32[]{:S(2)}) collective-permute-start(f32[128,768]{1,0:T(8,128)S(1)} %get-tuple-element.31), channel_id=1, source_target_pairs={{0,1},{1,0},{2,3},{3,2},{4,5},{5,4},{6,7},{7,6},{8,9},{9,8},{10,11... | collective-permute-start | bytes 1179656 | tf_op jit(solution)/shard_map/ppermute | solution.py:218
  147.9 16.3 %collective-permute-start.36 = (f32[128,768]{1,0:T(8,128)S(1)}, f32[128,768]{1,0:T(8,128)S(1)}, u32[]{:S(2)}, u32[]{:S(2)}) collective-permute-start(f32[128,768]{1,0:T(8,128)S(1)} %add.156), channel_id=1, source_target_pairs={{0,2},{1,3},{6,4},{7,5},{8,10},{9,11},{14,12},{15,13},{16,18},{17,... | collective-permute-start | bytes 1179656 | tf_op jit(solution)/shard_map/ppermute | solution.py:373
  149.3 23.4 %collective-permute-start.31 = (f32[128,768]{1,0:T(8,128)S(1)}, f32[128,768]{1,0:T(8,128)S(1)}, u32[]{:S(2)}, u32[]{:S(2)}) collective-permute-start(f32[128,768]{1,0:T(8,128)S(1)} %add.151), channel_id=1, source_target_pairs={{0,2},{1,3},{6,4},{7,5},{8,10},{9,11},{14,12},{15,13},{16,18},{17,... | collective-permute-start | bytes 1179656 | tf_op jit(solution)/shard_map/ppermute | solution.py:373
  150.7 30.4 %collective-permute-start.26 = (f32[128,768]{1,0:T(8,128)S(1)}, f32[128,768]{1,0:T(8,128)S(1)}, u32[]{:S(2)}, u32[]{:S(2)}) collective-permute-start(f32[128,768]{1,0:T(8,128)S(1)} %add.146), channel_id=1, source_target_pairs={{0,2},{1,3},{6,4},{7,5},{8,10},{9,11},{14,12},{15,13},{16,18},{17,... | collective-permute-start | bytes 1179656 | tf_op jit(solution)/shard_map/ppermute | solution.py:373
  152.3 37.2 %collective-permute-start.21 = (f32[128,768]{1,0:T(8,128)S(1)}, f32[128,768]{1,0:T(8,128)S(1)}, u32[]{:S(2)}, u32[]{:S(2)}) collective-permute-start(f32[128,768]{1,0:T(8,128)S(1)} %add.141), channel_id=1, source_target_pairs={{0,2},{1,3},{6,4},{7,5},{8,10},{9,11},{14,12},{15,13},{16,18},{17,... | collective-permute-start | bytes 1179656 | tf_op jit(solution)/shard_map/ppermute | solution.py:373
  164.2 33.5 %collective-permute-start.11 = (f32[128,768]{1,0:T(8,128)S(1)}, f32[128,768]{1,0:T(8,128)S(1)}, u32[]{:S(2)}, u32[]{:S(2)}) collective-permute-start(f32[128,768]{1,0:T(8,128)S(1)} %add.131), channel_id=1, source_target_pairs={{0,2},{1,3},{6,4},{7,5},{8,10},{9,11},{14,12},{15,13},{16,18},{17,... | collective-permute-start | bytes 1179656 | tf_op jit(solution)/shard_map/ppermute | solution.py:373
  172.7 25.8 %collective-permute-start.37 = (f32[128,768]{1,0:T(8,128)S(1)}, f32[128,768]{1,0:T(8,128)S(1)}, u32[]{:S(2)}, u32[]{:S(2)}) collective-permute-start(f32[128,768]{1,0:T(8,128)S(1)} %add.157), channel_id=1, source_target_pairs={{2,4},{3,5},{4,2},{5,3},{10,12},{11,13},{12,10},{13,11},{18,20},{1... | collective-permute-start | bytes 1179656 | tf_op jit(solution)/shard_map/ppermute | solution.py:373
  173.4 25.8 %collective-permute-start.32 = (f32[128,768]{1,0:T(8,128)S(1)}, f32[128,768]{1,0:T(8,128)S(1)}, u32[]{:S(2)}, u32[]{:S(2)}) collective-permute-start(f32[128,768]{1,0:T(8,128)S(1)} %add.152), channel_id=1, source_target_pairs={{2,4},{3,5},{4,2},{5,3},{10,12},{11,13},{12,10},{13,11},{18,20},{1... | collective-permute-start | bytes 1179656 | tf_op jit(solution)/shard_map/ppermute | solution.py:373
  181.1 23.6 %collective-permute-start.17 = (f32[128,1024]{1,0:T(8,128)S(1)}, f32[128,1024]{1,0:T(8,128)S(1)}, u32[]{:S(2)}, u32[]{:S(2)}) collective-permute-start(f32[128,1024]{1,0:T(8,128)S(1)} %add.137), channel_id=1, source_target_pairs={{2,4},{3,5},{4,2},{5,3},{10,12},{11,13},{12,10},{13,11},{18,20},{1... | collective-permute-start | bytes 1572872 | tf_op jit(solution)/shard_map/ppermute | solution.py:373
  189.5 11.1 %collective-permute-start.27 = (f32[128,768]{1,0:T(8,128)S(1)}, f32[128,768]{1,0:T(8,128)S(1)}, u32[]{:S(2)}, u32[]{:S(2)}) collective-permute-start(f32[128,768]{1,0:T(8,128)S(1)} %add.147), channel_id=1, source_target_pairs={{2,4},{3,5},{4,2},{5,3},{10,12},{11,13},{12,10},{13,11},{18,20},{1... | collective-permute-start | bytes 1179656 | tf_op jit(solution)/shard_map/ppermute | solution.py:373
  197.7 4.2 %collective-permute-start.22 = (f32[128,768]{1,0:T(8,128)S(1)}, f32[128,768]{1,0:T(8,128)S(1)}, u32[]{:S(2)}, u32[]{:S(2)}) collective-permute-start(f32[128,768]{1,0:T(8,128)S(1)} %add.142), channel_id=1, source_target_pairs={{2,4},{3,5},{4,2},{5,3},{10,12},{11,13},{12,10},{13,11},{18,20},{1... | collective-permute-start | bytes 1179656 | tf_op jit(solution)/shard_map/ppermute | solution.py:373
  198.5 4.9 %collective-permute-start.12 = (f32[128,768]{1,0:T(8,128)S(1)}, f32[128,768]{1,0:T(8,128)S(1)}, u32[]{:S(2)}, u32[]{:S(2)}) collective-permute-start(f32[128,768]{1,0:T(8,128)S(1)} %add.132), channel_id=1, source_target_pairs={{2,4},{3,5},{4,2},{5,3},{10,12},{11,13},{12,10},{13,11},{18,20},{1... | collective-permute-start | bytes 1179656 | tf_op jit(solution)/shard_map/ppermute | solution.py:373
  199.2 16.9 %collective-permute-start.38 = (f32[128,768]{1,0:T(8,128)S(1)}, f32[128,768]{1,0:T(8,128)S(1)}, u32[]{:S(2)}, u32[]{:S(2)}) collective-permute-start(f32[128,768]{1,0:T(8,128)S(1)} %add.159), channel_id=1, source_target_pairs={{4,6},{5,7},{2,0},{3,1},{12,14},{13,15},{10,8},{11,9},{20,22},{21,... | collective-permute-start | bytes 1179656 | tf_op jit(solution)/shard_map/ppermute | solution.py:373
  200.6 24.6 %collective-permute-start.33 = (f32[128,768]{1,0:T(8,128)S(1)}, f32[128,768]{1,0:T(8,128)S(1)}, u32[]{:S(2)}, u32[]{:S(2)}) collective-permute-start(f32[128,768]{1,0:T(8,128)S(1)} %add.154), channel_id=1, source_target_pairs={{4,6},{5,7},{2,0},{3,1},{12,14},{13,15},{10,8},{11,9},{20,22},{21,... | collective-permute-start | bytes 1179656 | tf_op jit(solution)/shard_map/ppermute | solution.py:373
  202.0 31.7 %collective-permute-start.28 = (f32[128,768]{1,0:T(8,128)S(1)}, f32[128,768]{1,0:T(8,128)S(1)}, u32[]{:S(2)}, u32[]{:S(2)}) collective-permute-start(f32[128,768]{1,0:T(8,128)S(1)} %add.149), channel_id=1, source_target_pairs={{4,6},{5,7},{2,0},{3,1},{12,14},{13,15},{10,8},{11,9},{20,22},{21,... | collective-permute-start | bytes 1179656 | tf_op jit(solution)/shard_map/ppermute | solution.py:373
  203.3 58.5 %collective-permute-start.23 = (f32[128,768]{1,0:T(8,128)S(1)}, f32[128,768]{1,0:T(8,128)S(1)}, u32[]{:S(2)}, u32[]{:S(2)}) collective-permute-start(f32[128,768]{1,0:T(8,128)S(1)} %add.144), channel_id=1, source_target_pairs={{4,6},{5,7},{2,0},{3,1},{12,14},{13,15},{10,8},{11,9},{20,22},{21,... | collective-permute-start | bytes 1179656 | tf_op jit(solution)/shard_map/ppermute | solution.py:373
  204.7 57.8 %collective-permute-start.13 = (f32[128,768]{1,0:T(8,128)S(1)}, f32[128,768]{1,0:T(8,128)S(1)}, u32[]{:S(2)}, u32[]{:S(2)}) collective-permute-start(f32[128,768]{1,0:T(8,128)S(1)} %add.134), channel_id=1, source_target_pairs={{4,6},{5,7},{2,0},{3,1},{12,14},{13,15},{10,8},{11,9},{20,22},{21,... | collective-permute-start | bytes 1179656 | tf_op jit(solution)/shard_map/ppermute | solution.py:373
  216.1 45.6 %collective-permute-start.18 = (f32[128,1024]{1,0:T(8,128)S(1)}, f32[128,1024]{1,0:T(8,128)S(1)}, u32[]{:S(2)}, u32[]{:S(2)}) collective-permute-start(f32[128,1024]{1,0:T(8,128)S(1)} %add.139), channel_id=1, source_target_pairs={{4,6},{5,7},{2,0},{3,1},{12,14},{13,15},{10,8},{11,9},{20,22},{21,... | collective-permute-start | bytes 1572872 | tf_op jit(solution)/shard_map/ppermute | solution.py:373
  225.2 45.9 %collective-permute-start.39 = (f32[128,768]{1,0:T(8,128)S(1)}, f32[128,768]{1,0:T(8,128)S(1)}, u32[]{:S(2)}, u32[]{:S(2)}) collective-permute-start(f32[128,768]{1,0:T(8,128)S(1)} %add_add_fusion.1.mine_ref), channel_id=1, source_target_pairs={{0,1},{1,0},{2,3},{3,2},{4,5},{5,4},{6,7},{7,6},{8,9},{9,8},{10,11... | collective-permute-start | bytes 1179656 | tf_op jit(solution)/shard_map/ppermute | solution.py:218
  225.2 43.5 %slice-start = ((s8[4718592]{0:T(1024)(128)(4,1)}), s8[4194304]{0:T(1024)(128)(4,1)S(1)}, s32[]{:S(2)}) async-start(s8[4718592]{0:T(1024)(128)(4,1)} %bitcast.10), calls=%async_computation.2 | async-start | bytes 8388608
  233.6 39.8 %collective-permute-start.34 = (f32[128,768]{1,0:T(8,128)S(1)}, f32[128,768]{1,0:T(8,128)S(1)}, u32[]{:S(2)}, u32[]{:S(2)}) collective-permute-start(f32[128,768]{1,0:T(8,128)S(1)} %add_add_fusion.2.mine_ref), channel_id=1, source_target_pairs={{0,1},{1,0},{2,3},{3,2},{4,5},{5,4},{6,7},{7,6},{8,9},{9,8},{10,11... | collective-permute-start | bytes 1179656 | tf_op jit(solution)/shard_map/ppermute | solution.py:218
  261.7 14.1 %collective-permute-start.29 = (f32[128,768]{1,0:T(8,128)S(1)}, f32[128,768]{1,0:T(8,128)S(1)}, u32[]{:S(2)}, u32[]{:S(2)}) collective-permute-start(f32[128,768]{1,0:T(8,128)S(1)} %add_add_fusion.3.mine_ref), channel_id=1, source_target_pairs={{0,1},{1,0},{2,3},{3,2},{4,5},{5,4},{6,7},{7,6},{8,9},{9,8},{10,11... | collective-permute-start | bytes 1179656 | tf_op jit(solution)/shard_map/ppermute | solution.py:218
  261.8 2.4 collective-permute-start.19
  262.5 6.2 %slice-start.1 = ((s8[4718592]{0:T(1024)(128)(4,1)}), s8[524288]{0:T(1024)(128)(4,1)S(1)}, s32[]{:S(2)}) async-start(s8[4718592]{0:T(1024)(128)(4,1)} %bitcast.10), calls=%async_computation.3 | async-start | bytes 1048576
  262.5 15.8 %collective-permute-start.24 = (f32[128,768]{1,0:T(8,128)S(1)}, f32[128,768]{1,0:T(8,128)S(1)}, u32[]{:S(2)}, u32[]{:S(2)}) collective-permute-start(f32[128,768]{1,0:T(8,128)S(1)} %add_add_fusion.4.mine_ref), channel_id=1, source_target_pairs={{0,1},{1,0},{2,3},{3,2},{4,5},{5,4},{6,7},{7,6},{8,9},{9,8},{10,11... | collective-permute-start | bytes 1179656 | tf_op jit(solution)/shard_map/ppermute | solution.py:218
  264.2 16.4 %collective-permute-start.14 = (f32[128,768]{1,0:T(8,128)S(1)}, f32[128,768]{1,0:T(8,128)S(1)}, u32[]{:S(2)}, u32[]{:S(2)}) collective-permute-start(f32[128,768]{1,0:T(8,128)S(1)} %add_add_fusion.5.mine_ref), channel_id=1, source_target_pairs={{0,1},{1,0},{2,3},{3,2},{4,5},{5,4},{6,7},{7,6},{8,9},{9,8},{10,11... | collective-permute-start | bytes 1179656 | tf_op jit(solution)/shard_map/ppermute | solution.py:218
  (6 other events, 6.2 us)

commit v2 on v1

v2 whole, which is shorter than its diff:
```python
import functools
import jax
import jax.numpy as jnp
from jax import lax
from jax.experimental import pallas as pl
from jax.experimental.pallas import tpu as pltpu
from jax.sharding import PartitionSpec as P

K = 256
G = 18432
PENALTY = float(G * K) / 64.0
EXTRA = 8
HALVES = 2
VMEM = 48 * 1024 * 1024
MINOR = (((1,), (1,)), ((), ()))
PLAIN = (((1,), (0,)), ((), ()))
F32 = jnp.float32
BF16 = jnp.bfloat16


def dot(a, b, dims, precision=None):
    return lax.dot_general(a, b, dims, precision=precision, preferred_element_type=F32)


def kernel_call(body, out_shape, flops, nbytes, **kw):
    return pl.pallas_call(
        body,
        out_shape=out_shape,
        compiler_params=pltpu.CompilerParams(vmem_limit_bytes=VMEM),
        cost_estimate=pl.CostEstimate(flops=int(flops), bytes_accessed=int(nbytes), transcendentals=0),
        **kw,
    )


def shape(*dims, dtype=F32):
    return jax.ShapeDtypeStruct(dims, dtype)


SMEM_SPEC = pl.BlockSpec(memory_space=pltpu.SMEM)


def pack(factors, position, me, width, bins):
    rows, width_all = factors.shape
    group = rows // bins
    lanes = 128 if width_all % 128 == 0 and 128 % width == 0 else width_all

    def body(me_ref, fac_ref, pos_ref, out_ref, turned):
        turned[...] = fac_ref[...].T
        first = pl.multiple_of(lax.rem(me_ref[0] * width, lanes), width)
        out_ref[0, :width, :] = turned[pl.ds(first, width), :]
        out_ref[0, width:, :] = jnp.broadcast_to(pos_ref[0], (EXTRA, group))

    grid_spec = pltpu.PrefetchScalarGridSpec(
        num_scalar_prefetch=1,
        grid=(bins,),
        in_specs=[
            pl.BlockSpec((group, lanes), lambda t, m: (t, m[0] * width // lanes)),
            pl.BlockSpec((1, 1, group), lambda t, m: (t, 0, 0)),
        ],
        out_specs=pl.BlockSpec((1, width + EXTRA, group), lambda t, m: (t, 0, 0)),
        scratch_shapes=[pltpu.VMEM((lanes, group), F32)],
    )
    return kernel_call(
        body, shape(bins, width + EXTRA, group), 0, 6 * rows * width * 4, grid_spec=grid_spec
    )(me, factors, position.astype(F32).reshape(bins, 1, group))


def to_grid(got, edge_codes, bin_me):
    bins, wide, group = got.shape
    width = wide - EXTRA
    grid_rows, grid_cols = edge_codes.shape
    rows = bins * group

    def body(me_ref, got_ref, code_ref, grid_ref, first_ref, last_ref, cell_ref, masked):
        block = jnp.concatenate([got_ref[s] for s in range(bins)], axis=1)
        cell = block[width : width + 1].astype(jnp.int32) - me_ref[0] * rows
        cell_ref[...] = cell
        at_row, at_col = cell // grid_cols, cell % grid_cols
        col_hot = jnp.where(
            lax.broadcasted_iota(jnp.int32, (grid_cols, rows), 0) == at_col, 1.0, 0.0
        ).astype(BF16)
        values = block[:width]
        high = values.astype(BF16)
        both = jnp.concatenate([high, (values - high.astype(F32)).astype(BF16)], axis=0)
        for r in range(grid_rows):
            mask = jnp.where(at_row == r, 1.0, 0.0).astype(BF16)
            masked[r * 2 * width : (r + 1) * 2 * width, :] = both * mask
        placed = dot(masked[...], col_hot, MINOR)
        scale = code_ref[...].astype(F32) / 8.0
        for r in range(grid_rows):
            at = r * 2 * width
            line = placed[at : at + width] + placed[at + width : at + 2 * width]
            row_scale = scale[r : r + 1]
            weighted = jnp.concatenate(
                [line * row_scale, jnp.broadcast_to(row_scale, (EXTRA, grid_cols))], axis=0
            )
            grid_ref[r] = weighted
            if r == 0:
                first_ref[...] = weighted
            if r == grid_rows - 1:
                last_ref[...] = weighted

    vm = pl.BlockSpec(memory_space=pltpu.VMEM)
    return kernel_call(
        body,
        (
            shape(grid_rows, wide, grid_cols),
            shape(wide, grid_cols),
            shape(wide, grid_cols),
            shape(1, rows, dtype=jnp.int32),
        ),
        4 * rows * rows * width,
        8 * rows * wide,
        in_specs=[SMEM_SPEC, vm, vm],
        out_specs=(vm, vm, vm, vm),
        scratch_shapes=[pltpu.VMEM((grid_rows * 2 * width, rows), BF16)],
    )(bin_me, got, edge_codes)


def from_grid(grid, above, below, cell, edge_codes, bins):
    grid_rows, wide, grid_cols = grid.shape
    rows = cell.shape[1]
    group = rows // bins

    def body(grid_ref, above_ref, below_ref, cell_ref, code_ref, out_ref, halves):
        scale = code_ref[...].astype(F32) / 8.0
        lane = lax.broadcasted_iota(jnp.int32, (wide, grid_cols), 1)
        for r in range(grid_rows):
            here = grid_ref[r]
            upper = above_ref[...] if r == 0 else grid_ref[r - 1]
            lower = below_ref[...] if r == grid_rows - 1 else grid_ref[r + 1]
            left = jnp.where(lane == 0, 0.0, pltpu.roll(here, 1, 1))
            right = jnp.where(lane == grid_cols - 1, 0.0, pltpu.roll(here, grid_cols - 1, 1))
            value = scale[r : r + 1] * (left + right + 0.5 * (upper + lower))
            high = value.astype(BF16)
            halves[r * wide : (r + 1) * wide, :grid_cols] = high
            halves[r * wide : (r + 1) * wide, grid_cols:] = (value - high.astype(F32)).astype(BF16)
        cell = cell_ref[...]
        at_row, at_col = cell // grid_cols, cell % grid_cols
        for s in range(bins // 2):
            lo, hi = 2 * s * group, (2 * s + 2) * group
            hot = jnp.where(
                lax.broadcasted_iota(jnp.int32, (grid_cols, hi - lo), 0) == at_col[:, lo:hi], 1.0, 0.0
            ).astype(BF16)
            lines = dot(halves[...], jnp.concatenate([hot, hot], axis=0), PLAIN)
            row_here = at_row[:, lo:hi]
            total = jnp.zeros((wide, hi - lo), F32)
            for r in range(grid_rows):
                total = total + jnp.where(row_here == r, lines[r * wide : (r + 1) * wide], 0.0)
            out_ref[2 * s] = total[:, :group]
            out_ref[2 * s + 1] = total[:, group:]

    vm = pl.BlockSpec(memory_space=pltpu.VMEM)
    return kernel_call(
        body,
        shape(bins, wide, group),
        4 * rows * rows * wide,
        8 * rows * wide,
        in_specs=[vm] * 5,
        out_specs=vm,
        scratch_shapes=[pltpu.VMEM((grid_rows * wide, 2 * grid_cols), BF16)],
    )(grid, above, below, cell, edge_codes)


def numer_part(counts, loadings, me, genes_n, half, send_ids, with_gram):
    rows, genes = counts.shape
    width_all = loadings.shape[0]
    width = width_all // genes_n
    step = 512
    steps = rows // 2 // step
    keep_ids = [k for k in range(genes_n) if k not in send_ids]
    total_cols = steps * step + with_gram * width_all
    first_call = loadings.dtype == F32

    def body(me_ref, counts_ref, load_ref, send_ref, keep_ref, *rest):
        at = pl.program_id(0)
        load_bf = rest[0] if first_call else load_ref
        firsts = [pl.multiple_of((k ^ me_ref[0]) * width, width) for k in range(genes_n)]

        if first_call:

            @pl.when(at == 0)
            def _():
                for k, first in enumerate(firsts):
                    load_bf[k * width : (k + 1) * width, :] = load_ref[pl.ds(first, width), :].astype(BF16)

        def put(part, cols):
            for i, k in enumerate(send_ids):
                send_ref[i, :, cols] = part[k * width : (k + 1) * width]
            for i, k in enumerate(keep_ids):
                keep_ref[i, :, cols] = part[k * width : (k + 1) * width]

        put(dot(counts_ref[...], load_bf[...], MINOR).T, pl.ds(pl.multiple_of(at * step, step), step))

        if with_gram:
            turned = rest[-1]

            @pl.when(at == steps - 1)
            def _():
                local = dot(load_bf[...], load_bf[...], MINOR)
                for k, first in enumerate(firsts):
                    turned[pl.ds(first, width), :] = local[k * width : (k + 1) * width]
                put(turned[...].T, slice(steps * step, total_cols))

    out = shape(genes_n // 2, width, total_cols)
    out_spec = pl.BlockSpec(out.shape, lambda i, m: (0, 0, 0))
    load_spec = pl.BlockSpec((width_all, genes), lambda i, m: (0, 0))
    grid_spec = pltpu.PrefetchScalarGridSpec(
        num_scalar_prefetch=1,
        grid=(steps,),
        in_specs=[pl.BlockSpec((step, genes), lambda i, m: (i + half * steps, 0)), load_spec],
        out_specs=(out_spec, out_spec) + (load_spec,) * first_call,
        scratch_shapes=[pltpu.VMEM((width_all, width_all), F32)] * with_gram,
    )
    return kernel_call(
        body,
        (out, out) + (shape(width_all, genes, dtype=BF16),) * first_call,
        2 * total_cols * genes * width_all,
        rows * genes + 4 * genes * width_all + 4 * total_cols * width_all,
        grid_spec=grid_spec,
    )(me, counts, loadings)


def swap(block, axis, bit):
    return lax.ppermute(block, axis, [(i, i ^ bit) for i in range(lax.axis_size(axis))])


def picked_sum(arrays, ids):
    _, width, cols = arrays[0].shape

    def body(*refs):
        total = refs[0][...]
        for ref in refs[1:-1]:
            total = total + ref[...]
        refs[-1][...] = total

    first, step = ids[0], (ids[1] - ids[0] if len(ids) > 1 else 1)
    return kernel_call(
        body,
        shape(len(ids), width, cols),
        0,
        4 * (len(arrays) + 1) * len(ids) * width * cols,
        grid=(len(ids),),
        in_specs=[pl.BlockSpec((1, width, cols), lambda i: (first + step * i, 0, 0))] * len(arrays),
        out_specs=pl.BlockSpec((1, width, cols), lambda i: (i, 0, 0)),
    )(*arrays)


def scatter_sum(send, keep, keep_ids, bits):
    arrays = [keep, swap(send, "gene", bits[0])]
    for bit in bits[1:]:
        out_ids = [i for i, k in enumerate(keep_ids) if k & bit]
        in_ids = [i for i, k in enumerate(keep_ids) if not k & bit]
        got = swap(picked_sum(arrays, out_ids), "gene", bit)
        if len(in_ids) == 1:
            arrays = arrays + [got]
        else:
            arrays = [picked_sum(arrays, in_ids), got]
        keep_ids = [keep_ids[i] for i in in_ids]
    return arrays


def plain_terms(numer, factors, rows, width):
    width_all = factors.shape[1]
    half_rows = rows // 2
    counts_in = [len(x) for x in numer]

    def body(*refs):
        parts = (refs[: counts_in[0]], refs[counts_in[0] : sum(counts_in)])
        fac_ref, numer_ref, plain_ref, gram = refs[-4:]
        at = pl.program_id(0)

        def total(half, cols):
            out = parts[half][0][0, :, cols]
            for ref in parts[half][1:]:
                out = out + ref[0, :, cols]
            return out

        @pl.when(at == 0)
        def _():
            gram[...] = total(0, slice(half_rows, half_rows + width_all))
            numer_ref[...] = total(0, slice(0, half_rows))

        @pl.when(at == 1)
        def _():
            numer_ref[...] = total(1, slice(0, half_rows))

        plain_ref[...] = dot(fac_ref[...], gram[...], MINOR, lax.Precision.HIGHEST).T

    whole = lambda x: pl.BlockSpec((1,) + x.shape[1:], lambda i: (0, 0, 0))
    out_spec = pl.BlockSpec((width, half_rows), lambda i: (0, i))
    arrays = list(numer[0]) + list(numer[1])
    return kernel_call(
        body,
        (shape(width, rows),) * 2,
        12 * width * width_all * rows,
        4 * rows * (width_all + 5 * width),
        grid=(2,),
        in_specs=[whole(x) for x in arrays] + [pl.BlockSpec((half_rows, width_all), lambda i: (i, 0))],
        out_specs=(out_spec, out_spec),
        scratch_shapes=[pltpu.VMEM((width, width_all), F32)],
    )(*arrays, factors)


def new_factors(payload, back, numer, plain):
    bins, wide, group = payload.shape
    width = wide - EXTRA

    def body(pay_ref, back_ref, numer_ref, plain_ref, out_ref):
        pay = jnp.concatenate([pay_ref[s] for s in range(bins)], axis=1)
        got = jnp.concatenate([back_ref[s] for s in range(bins)], axis=1)
        fac, smooth, degree = pay[:width], got[:width], got[width : width + 1]
        out_ref[...] = (
            fac * (numer_ref[...] + PENALTY * smooth) / (plain_ref[...] + PENALTY * degree * fac)
        )

    vm = pl.BlockSpec(memory_space=pltpu.VMEM)
    return kernel_call(
        body,
        shape(width, bins * group),
        0,
        4 * 5 * wide * bins * group,
        in_specs=[vm] * 4,
        out_specs=vm,
    )(payload, back, numer, plain)


def halves_out(blocks, token):
    width, rows = blocks[0][0].shape
    half_rows = rows // 2

    def body(*refs):
        n = len(blocks)
        for src, dst in zip(refs[:n], refs[n + 1 :]):
            dst[...] = src[...]

    spec = lambda half: pl.BlockSpec((width, half_rows), lambda i: (0, half))
    return kernel_call(
        body,
        (shape(width, half_rows),) * len(blocks),
        0,
        8 * len(blocks) * width * half_rows,
        grid=(1,),
        in_specs=[spec(h) for _, h in blocks] + [pl.BlockSpec(memory_space=pl.ANY)],
        out_specs=tuple(spec(0) for _ in blocks),
    )(*[b for b, _ in blocks], token)


def turned_back(blocks, ids, width, me, token):
    arrays = [x for b in blocks for x in b]
    rows = sum(x.shape[1] for x in blocks[0])
    width_all = len(ids) * width
    step = 384
    steps = rows // step

    def body(me_ref, *refs):
        out_ref, block = refs[-2:]
        at = pl.program_id(0)
        pos = 0
        for b, k in zip(blocks, ids):
            first = pl.multiple_of((k ^ me_ref[0]) * width, width)
            if len(b) == 1:
                block[pl.ds(first, width), :] = refs[pos][...]
            else:
                block[pl.ds(first, width), :] = jnp.where(at < steps // 2, refs[pos][...], refs[pos + 1][...])
            pos += len(b)
        out_ref[...] = block[...].T

    specs = []
    for b in blocks:
        if len(b) == 1:
            specs.append(pl.BlockSpec((width, step), lambda i, m: (0, i)))
        else:
            specs.append(pl.BlockSpec((width, step), lambda i, m: (0, jnp.minimum(i, steps // 2 - 1))))
            specs.append(pl.BlockSpec((width, step), lambda i, m: (0, jnp.maximum(i - steps // 2, 0))))
    grid_spec = pltpu.PrefetchScalarGridSpec(
        num_scalar_prefetch=1,
        grid=(steps,),
        in_specs=specs + [pl.BlockSpec(memory_space=pl.ANY)],
        out_specs=pl.BlockSpec((step, width_all), lambda i, m: (i, 0)),
        scratch_shapes=[pltpu.VMEM((width_all, step), F32)],
    )
    return kernel_call(
        body, shape(rows, width_all), 0, 8 * rows * width_all, grid_spec=grid_spec
    )(me, *arrays, token)


def cross_part(blocks, n_old, counts, flags, half, with_gram, width_all, token):
    arrays = [x for b in blocks for x in b]
    width = arrays[0].shape[0]
    rows, genes = counts.shape
    cols = genes // HALVES
    steps = 3
    step = cols // steps
    n_new = len(blocks) - n_old
    extra = width_all if with_gram else 0
    part = width // 2

    def body(flag_ref, counts_ref, *refs):
        send_ref, keep_ref, fac = refs[-3:]
        at = pl.program_id(0)
        core = flag_ref[1]

        @pl.when(at == 0)
        def _():
            pos = 0
            for j, b in enumerate(blocks):
                col = 0
                for x in b:
                    fac[j * width : (j + 1) * width, col : col + x.shape[1]] = refs[pos][...].astype(BF16)
                    col += x.shape[1]
                    pos += 1

        def put(result, where):
            for i in range(n_new):
                lo = result[i * width : i * width + part]
                hi = result[i * width + part : (i + 1) * width]
                send_ref[i, :, where] = jnp.where(core == 0, hi, lo)
                keep_ref[i, :, where] = jnp.where(core == 0, lo, hi)

        new = fac[n_old * width :, :]
        put(dot(new, counts_ref[...], PLAIN), pl.ds(pl.multiple_of(at * step, step), step))

        if with_gram:

            @pl.when(at == 0)
            def _():
                near = dot(new, fac[...], MINOR)
                if near.shape[1] < width_all:
                    gap = jnp.zeros((near.shape[0], width_all - near.shape[1]), F32)
                    near = jnp.concatenate([near, gap], axis=1)
                put(near, slice(cols, cols + extra))

    out = shape(n_new, part, cols + extra)
    out_spec = pl.BlockSpec(out.shape, lambda i, f: (0, 0, 0))
    grid_spec = pltpu.PrefetchScalarGridSpec(
        num_scalar_prefetch=1,
        grid=(steps,),
        in_specs=[pl.BlockSpec((rows, step), lambda i, f: (0, half * steps + i))]
        + [pl.BlockSpec(x.shape, lambda i, f: (0, 0)) for x in arrays]
        + [pl.BlockSpec(memory_space=pl.ANY)],
        out_specs=(out_spec, out_spec),
        scratch_shapes=[pltpu.VMEM((len(blocks) * width, rows), BF16)],
    )
    return kernel_call(
        body,
        (out, out),
        2 * rows * n_new * width * (cols + extra),
        2 * rows * cols + 4 * rows * len(blocks) * width + 8 * n_new * part * (cols + extra),
        grid_spec=grid_spec,
    )(flags, counts, *arrays, token)


def line_slot(flags, t, chunks, own, got, token):
    line = lax.axis_size("bin") // 2
    right = [z for z in range(line - 1) if 0 <= t - z < chunks]
    left = [line - 1 - z for z in right]
    merged = not set(right) & set(left) and not {z + 1 for z in right} & {z - 1 for z in left}
    need = sorted({t - z for z in right})
    _, part, cols = own[need[0]][0].shape

    def body(flag_ref, *refs):
        z = flag_ref[2]
        come = dict(zip(("right", "left"), refs[2 * len(need) :]))
        outs = refs[-1:] * 2 if merged else refs[-2:]
        for name, active, out in (("right", right, outs[0]), ("left", left, outs[1])):
            for place in active:
                c = t - (place if name == "right" else line - 1 - place)
                a, b = refs[2 * need.index(c)], refs[2 * need.index(c) + 1]

                @pl.when(z == place)
                def _():
                    value = a[0] + b[0]
                    if c != t:
                        value = value + come[name][...]
                    out[...] = value

    block = lambda i: pl.BlockSpec((1, part, cols), lambda g, f: (i, 0, 0))
    flat = pl.BlockSpec((part, cols), lambda g, f: (0, 0))
    operands, specs = [], []
    for c in need:
        keep, came, i = own[c]
        operands += [keep, came]
        specs += [block(i)] * 2
    if got is not None:
        operands += list(got)
        specs += [flat] * 2
    operands.append(token)
    specs.append(pl.BlockSpec(memory_space=pl.ANY))
    n_out = 1 if merged else 2
    sends = kernel_call(
        body,
        (shape(part, cols),) * n_out,
        0,
        4 * part * cols * (len(operands) + n_out),
        grid_spec=pltpu.PrefetchScalarGridSpec(
            num_scalar_prefetch=1, grid=(1,), in_specs=specs, out_specs=(flat,) * n_out
        ),
    )(flags, *operands)
    pairs = lambda hops: [(2 * a + c, 2 * b + c) for a, b in hops for c in range(2)]
    to_right = pairs([(z, z + 1) for z in right])
    to_left = pairs([(z, z - 1) for z in left])
    if merged:
        come = lax.ppermute(sends[0], "bin", to_right + to_left)
        return (come, come), sends[0]
    return (lax.ppermute(sends[0], "bin", to_right), lax.ppermute(sends[1], "bin", to_left)), sends[1]


def line_total(flags, own, come, token):
    line = lax.axis_size("bin") // 2
    keep, came, index = own
    _, part, cols = keep.shape

    def body(flag_ref, a, b, *refs):
        out = refs[-1]
        z = flag_ref[2]
        out[...] = a[0] + b[0]
        for d in range(line - 1):

            @pl.when(z == d + 1)
            def _():
                out[...] += refs[2 * d][...]

            @pl.when(z == line - 2 - d)
            def _():
                out[...] += refs[2 * d + 1][...]

    block = pl.BlockSpec((1, part, cols), lambda g, f: (index, 0, 0))
    flat = pl.BlockSpec((part, cols), lambda g, f: (0, 0))
    operands = [keep, came] + [x for pair in come for x in pair] + [token]
    return kernel_call(
        body,
        shape(part, cols),
        0,
        4 * part * cols * len(operands),
        grid_spec=pltpu.PrefetchScalarGridSpec(
            num_scalar_prefetch=1,
            grid=(1,),
            in_specs=[block] * 2
            + [flat] * (2 * len(come))
            + [pl.BlockSpec(memory_space=pl.ANY)],
            out_specs=flat,
        ),
    )(flags, *operands)


def shares(loadings, totals, ids, flags, cols):
    width_all, genes = loadings.shape
    width = width_all // len(ids)
    part = width // 2
    extra = width_all
    steps = 6
    step = genes // steps

    def body(flag_ref, load_ref, *refs):
        out_ref, gram, load = refs[-3:]
        me, core = flag_ref[0], flag_ref[1]
        firsts = [pl.multiple_of((k ^ me) * width, width) for k in ids]

        @pl.when(pl.program_id(0) == 0)
        def _():
            for j in range(len(ids)):
                for ref, which in ((refs[2 * j], core), (refs[2 * j + 1], 1 - core)):
                    at = pl.multiple_of(j * width + which * part, part)
                    gram[pl.ds(at, part), :] = ref[...]
            low = gram[...]
            row = lax.broadcasted_iota(jnp.int32, low.shape, 0) // width
            col = lax.broadcasted_iota(jnp.int32, low.shape, 1) // width
            gram[...] = jnp.where(col <= row, low, low.T)

        for j, first in enumerate(firsts):
            load[j * width : (j + 1) * width, :] = load_ref[pl.ds(first, width), :]
        value = load[...]
        value = value / dot(gram[...], value, PLAIN, lax.Precision.HIGHEST)
        for j, first in enumerate(firsts):
            out_ref[pl.ds(first, width), :] = value[j * width : (j + 1) * width]

    gram_spec = pl.BlockSpec((part, extra), lambda i, f: (0, 0))
    block = pl.BlockSpec((width_all, step), lambda i, f: (0, i))
    pieces = [x[:, cols:] for pair in totals for x in pair]
    return kernel_call(
        body,
        shape(width_all, genes),
        12 * width_all * width_all * genes,
        8 * width_all * genes,
        grid_spec=pltpu.PrefetchScalarGridSpec(
            num_scalar_prefetch=1,
            grid=(steps,),
            in_specs=[block] + [gram_spec] * len(pieces),
            out_specs=block,
            scratch_shapes=[
                pltpu.VMEM((width_all, width_all), F32),
                pltpu.VMEM((width_all, step), F32),
            ],
        ),
    )(flags, loadings, *pieces)


def new_loadings(share, mine, other, k, half, width, flags, before):
    width_all, genes = share.shape
    cols = genes // HALVES
    part = width // 2

    def body(flag_ref, share_ref, mine_ref, other_ref, *rest):
        out_ref = rest[-1]
        for ref, which in ((mine_ref, flag_ref[1]), (other_ref, 1 - flag_ref[1])):
            at = pl.ds(pl.multiple_of(which * part, part), part)
            out_ref[at, :] = share_ref[at, :] * ref[...]

    rows_at = pl.BlockSpec((width, cols), lambda i, f: (k ^ f[0], half))
    flat = pl.BlockSpec((part, cols), lambda i, f: (0, 0))
    operands, specs, aliases = [flags, share, mine, other], [rows_at, flat, flat], {}
    if before is not None:
        operands.append(before)
        specs.append(pl.BlockSpec(memory_space=pl.ANY))
        aliases = {len(operands) - 1: 0}
    return kernel_call(
        body,
        shape(width_all, genes),
        0,
        16 * width * cols,
        grid_spec=pltpu.PrefetchScalarGridSpec(
            num_scalar_prefetch=1, grid=(1,), in_specs=specs, out_specs=rows_at
        ),
        input_output_aliases=aliases,
    )(*operands)


def on_device(counts, factors, loadings, position, edge_codes):
    bins, genes_n = lax.axis_size("bin"), lax.axis_size("gene")
    line = bins // 2
    me, bin_me = lax.axis_index("gene"), lax.axis_index("bin")
    rows, width_all = factors.shape
    genes = counts.shape[1]
    width = width_all // genes_n
    scalar = lambda x: jnp.asarray(x, jnp.int32).reshape(1)
    me1, bin1 = scalar(me), scalar(bin_me)
    flags = jnp.concatenate([me1, bin1 % 2, bin1 // 2])
    bits = [1 << b for b in range(genes_n.bit_length() - 1)]
    orders = (bits, bits[::-1])

    payload = pack(factors, position, me1, width, bins)
    got = lax.all_to_all(payload, "bin", split_axis=0, concat_axis=0, tiled=True)

    numer, load = [None, None], loadings
    for half in (1, 0):
        bit = orders[half][0]
        send_ids = [k for k in range(genes_n) if k & bit]
        keep_ids = [k for k in range(genes_n) if not k & bit]
        send, keep, *more = numer_part(counts, load, me1, genes_n, half, send_ids, half == 0)
        load = more[0] if more else load
        numer[half] = scatter_sum(send, keep, keep_ids, orders[half])

    grid, first, last, cell = to_grid(got, edge_codes, bin1)
    above = lax.ppermute(last, "bin", [(i, i + 1) for i in range(bins - 1)])
    below = lax.ppermute(first, "bin", [(i + 1, i) for i in range(bins - 1)])
    smooth = from_grid(grid, above, below, cell, edge_codes, bins)
    back = lax.all_to_all(smooth, "bin", split_axis=0, concat_axis=0, tiled=True)
    numer_own, plain = plain_terms(numer, factors, rows, width)
    own_block = new_factors(payload, back, numer_own, plain)

    ids = sorted(range(genes_n), key=lambda k: (bin(k).count("1"), k))
    groups = [[k for k in ids if bin(k).count("1") == n] for n in range(len(bits) + 1)]
    blocks = {0: (own_block,)}
    for k in bits:
        blocks[k] = (swap(own_block, "gene", k),)

    def come_on(group, token):
        for k in group:
            low, high = k & -k, 1 << (k.bit_length() - 1)
            pick = lambda b, h: (b[0], h) if len(b) == 1 else (b[h], None)
            sources = [pick(blocks[k ^ low], 0), pick(blocks[k ^ high], 1)]
            if sources[0][1] is not None:
                outs = halves_out(sources, token)
            else:
                outs = [s for s, _ in sources]
            blocks[k] = (swap(outs[0], "gene", low), swap(outs[1], "gene", high))
            token = outs[0]
        return token

    cols = genes // HALVES
    chunks = len(ids)
    own = [{} for _ in range(HALVES)]
    came = [[] for _ in range(HALVES)]
    totals = [{} for _ in range(HALVES)]
    token = own_block
    factors_new = None

    def product(group, half, token):
        upto = ids.index(group[-1]) + 1
        n_old = upto - len(group)
        send, keep = cross_part(
            [blocks[k] for k in ids[:upto]], n_old, counts, flags, half, half == 0, width_all, token
        )
        other = swap(send, "bin", 1)
        for i in range(len(group)):
            own[half][n_old + i] = (keep, other, i)
        return keep

    def finish(c, half, token):
        total = line_total(flags, own[half][c], came[half][c : c + line - 1], token)
        totals[half][c] = (total, swap(total, "bin", 1))
        return total

    for t in range(chunks + line - 2):
        for half in range(HALVES):
            if t < chunks and t not in own[half]:
                if t == 0 and half == 0:
                    for h in range(HALVES):
                        token = product(groups[0], h, token)
                else:
                    token = product(next(g for g in groups if ids[t] in g), half, token)
            sends, token = line_slot(
                flags, t, chunks, own[half], came[half][-1] if came[half] else None, token
            )
            came[half].append(sends)
        if t + 2 < len(groups):
            token = come_on(groups[t + 2], token)
        if t == chunks - 1:
            factors_new = turned_back([blocks[k] for k in ids], ids, width, me1, token)
            token = factors_new
        for half in range(HALVES):
            c = t - (line - 1)
            if 0 <= c < chunks:
                token = finish(c, half, token)
    for c in range(chunks):
        for half in range(HALVES):
            if c not in totals[half]:
                token = finish(c, half, token)
    share = shares(loadings, [totals[0][c] for c in range(chunks)], ids, flags, cols)
    loadings_new = None
    for c, k in enumerate(ids):
        for half in range(HALVES):
            mine, other = totals[half][c]
            loadings_new = new_loadings(share, mine, other, k, half, width, flags, loadings_new)
    return factors_new, loadings_new


def solution(mesh):
    placed = (P("bin", "gene"), P("bin", None), P(None, "gene"), P("bin"), P("bin", None))
    return jax.shard_map(
        on_device,
        mesh=mesh,
        in_specs=placed,
        out_specs=(P("bin", None), P(None, "gene")),
        check_vma=False,
    )
```

time: 284 us -> 306 us (1.077)
  waiting for transfers between devices: 138 us -> 99.9 us
  Pallas kernels: 80 us -> 114 us
  starting transfers between devices: 49.5 us -> 81.4 us
  other arithmetic: 7.09 us -> 0.79 us
    ppermute x18 -> x20, waiting for transfers between devices: 90.7 us -> 45.8 us  [the longest x4 21 us: line_slot(): come = lax.ppermute(sends[0], 'bin', to_right + to_left)]
    pallas_call x18 -> x43, Pallas kernels: 70.7 us -> 104 us  [the longest x6 44.3 us: cross_part(): kernel_call(body, (out, out), 2 * rows * n_new * width * (cols + extra),...]
    ppermute x18 -> x20, starting transfers between devices: 23 us -> 53 us  [the longest x8 33.8 us: line_slot(): lax.ppermute(sends[0], 'bin', to_right)]
    all_to_all x1, waiting for transfers between devices: 0.01 us -> 23.1 us  [on_device(): lax.all_to_all(payload, 'bin', split_axis=0, concat_axis=0, tiled=True)]
    ppermute x20 -> x22, waiting for transfers between devices: 39.5 us -> 31 us  [swap(): lax.ppermute(block, axis, [(i, i ^ bit) for i in range(lax.axis_size(axis...]
    add x28 -> x0, other arithmetic: 6.2 us -> none  [the longest x2 2.42 us: scatter_sum(): return keep[0] + got[0]]
    all_to_all x1, waiting for transfers between devices: 4.59 us -> 0.01 us  [on_device(): lax.all_to_all(smooth, 'bin', split_axis=0, concat_axis=0, tiled=True)]
    ppermute x20 -> x22, starting transfers between devices: 10.1 us -> 14 us  [swap(): lax.ppermute(block, axis, [(i, i ^ bit) for i in range(lax.axis_size(axis...]
  transfers between devices with their start and end apart: 42 -> 46, of which waited for: 18 -> 12; matrix products, arithmetic and copies ran while one was open for 2% -> 0% of each run, Pallas kernels for 23% -> 28%
where the time goes in v2:
time: 306 us; the launch traced here: 305 us
  Pallas kernels  114 us (37%)
  waiting for transfers between devices  99.9 us (33%)
  starting transfers between devices  81.4 us (27%)
  local copies, waits for them, and re-layouts  6.87 us (2%)
    pallas_call x6, Pallas kernels, cross_part(): kernel_call(body, (out, out), 2 * rows * n_new * width * (cols + extra),...  44.3 us
    ppermute x8, starting transfers between devices, line_slot(): lax.ppermute(sends[0], 'bin', to_right)  33.8 us
    ppermute x22, waiting for transfers between devices, swap(): lax.ppermute(block, axis, [(i, i ^ bit) for i in range(lax.axis_size(axis...  31 us
    all_to_all x1, waiting for transfers between devices, on_device(): lax.all_to_all(payload, 'bin', split_axis=0, concat_axis=0, tiled=True)  23.1 us
    ppermute x4, waiting for transfers between devices, line_slot(): come = lax.ppermute(sends[0], 'bin', to_right + to_left)  21 us
    ppermute x8, waiting for transfers between devices, line_slot(): lax.ppermute(sends[1], 'bin', to_left)  19.1 us
    pallas_call x2, Pallas kernels, numer_part(): kernel_call(body, (out, out) + (shape(width_all, genes, dtype=BF16),) * f...  17.9 us
    ppermute x22, starting transfers between devices, swap(): lax.ppermute(block, axis, [(i, i ^ bit) for i in range(lax.axis_size(axis...  14 us
  transfers between devices with their start and end apart: 46, of which 12 were waited for; matrix products, arithmetic and copies ran while one was open for 0% of the time, Pallas kernels for 28%

profile of v2, /device:TPU:0, one launch (start us, length us, event | category | flops | bytes accessed | tf_op | source)
XLA Modules:
  0.0 304.8 jit_solution(18432544714522423653)
XLA Ops:
  1.4 1.9 copy-done
  3.2 3.4 %shard_map.68.pay_ref = f32[8,72,384]{2,1,0:T(8,128)} custom-call(s32[1]{0:T(128)} %bitcast.me_ref, f32[3072,256]{1,0:T(8,128)S(1)} %copy-done, f32[8,1,384]{2,1,0:T(1,128)S(1)} %bitcast.3), custom_call_target="tpu_custom_call" | custom-call | bytes 4718592 | tf_op jit(solution)/shard_map/pallas_call | solution.py:63
  6.6 6.3 %all-to-all-start = ((f32[8,72,384]{2,1,0:T(8,128)}), f32[8,72,384]{2,1,0:T(8,128)S(1)}, u32[]{:S(2)}, u32[]{:S(2)}) async-start(f32[8,72,384]{2,1,0:T(8,128)} %shard_map.68.pay_ref), calls=%async_computation | async-start | bytes 1769472 | tf_op jit(solution)/shard_map/all_to_all | solution.py:643
  13.0 23.1 %all-to-all-done.got_ref = f32[8,72,384]{2,1,0:T(8,128)S(1)} async-done(((f32[8,72,384]{2,1,0:T(8,128)}), f32[8,72,384]{2,1,0:T(8,128)S(1)}, u32[]{:S(2)}, u32[]{:S(2)}) %all-to-all-start) | async-done | bytes 884768 | tf_op jit(solution)/shard_map/all_to_all | solution.py:643
  36.1 2.6 shard_map.69
  38.7 1.5 collective-permute-start
  41.6 9.3 %shard_map.71 = (f32[2,64,1536]{2,1,0:T(8,128)S(1)}, f32[2,64,1536]{2,1,0:T(8,128)S(1)}, bf16[256,4608]{1,0:T(8,128)(2,1)S(1)}) custom-call(s32[1]{0:T(128)} %bitcast.me_ref, bf16[3072,4608]{1,0:T(8,128)(2,1)} %counts_ref.15, f32[256,4608]{1,0:T(8,128)} %load_ref.3), custom_call_target="tpu_custom_call" | custom-call | flops 3623878656 | bytes 20447232 | tf_op jit(solution)/shard_map/pallas_call | solution.py:215
  52.3 4.2 %shard_map.70 = f32[8,72,384]{2,1,0:T(8,128)} custom-call(f32[12,72,256]{2,1,0:T(8,128)S(1)} %get-tuple-element.43.grid_ref, f32[72,256]{1,0:T(8,128)S(1)} %collective-permute-done.above_ref, f32[72,256]{1,0:T(8,128)S(1)} %collective-permute-done.1.below_ref, s32[1,3072]{1,0:T(1,128)S(1)} %get-tuple-element.46.cell_ref, s32[12,256]{1,0:T(8,128)S(1)} %copy-done.4), custom_call_target="tpu_custom_call" | custom-call | flops 2717908992 | bytes 1769472 | tf_op jit(solution)/shard_map/pallas_call | solution.py:154
  56.6 5.3 %all-to-all-start.1 = ((f32[8,72,384]{2,1,0:T(8,128)}), f32[8,72,384]{2,1,0:T(8,128)S(1)}, u32[]{:S(2)}, u32[]{:S(2)}) async-start(f32[8,72,384]{2,1,0:T(8,128)} %shard_map.70), calls=%async_computation.1 | async-start | bytes 1769472 | tf_op jit(solution)/shard_map/all_to_all | solution.py:658
  61.8 1.7 copy-done.3
  63.5 8.6 %shard_map.72 = (f32[2,64,1792]{2,1,0:T(8,128)S(1)}, f32[2,64,1792]{2,1,0:T(8,128)S(1)}) custom-call(s32[1]{0:T(128)} %bitcast.me_ref, bf16[3072,4608]{1,0:T(8,128)(2,1)} %counts_ref.15, bf16[256,4608]{1,0:T(8,128)(2,1)S(1)} %copy-done.3), custom_call_target="tpu_custom_call" | custom-call | flops 4227858432 | bytes 20709376 | tf_op jit(solution)/shard_map/pallas_call | solution.py:215
  72.1 1.6 collective-permute-start.2
  73.7 1.5 collective-permute-start.4
  75.2 19.8 %collective-permute-done.2.refs_1_ = f32[2,64,1792]{2,1,0:T(8,128)S(1)} collective-permute-done((f32[2,64,1792]{2,1,0:T(8,128)S(1)}, f32[2,64,1792]{2,1,0:T(8,128)S(1)}, u32[]{:S(2)}, u32[]{:S(2)}) %collective-permute-start.2) | collective-permute-done | bytes 917536 | tf_op jit(solution)/shard_map/ppermute | solution.py:225
  95.0 1.6 collective-permute-start.3
  96.6 1.6 collective-permute-start.5
  98.2 9.0 %collective-permute-done.5.refs_5_ = f32[1,64,1536]{2,1,0:T(8,128)S(1)} collective-permute-done((f32[1,64,1536]{2,1,0:T(8,128)S(1)}, f32[1,64,1536]{2,1,0:T(8,128)S(1)}, u32[]{:S(2)}, u32[]{:S(2)}) %collective-permute-start.5) | collective-permute-done | bytes 393248 | tf_op jit(solution)/shard_map/ppermute | solution.py:225
  107.2 4.5 %shard_map.75 = (f32[64,3072]{1,0:T(8,128)S(1)}, f32[64,3072]{1,0:T(8,128)S(1)}) custom-call(f32[2,64,1792]{2,1,0:T(8,128)S(1)} %get-tuple-element.48.refs_0_, f32[2,64,1792]{2,1,0:T(8,128)S(1)} %collective-permute-done.2.refs_1_, f32[1,64,1792]{2,1,0:T(8,128)S(1)} %collective-permute-done.3.refs_2_, f32[2,64,1536]{2,1,0:T(8,128)S(1)} %get-tuple-element.50.refs_0_.refs_3_, ...), custom_call_target="tpu_custom_call" | custom-call | flops 603979776 | bytes 7077888 | tf_op jit(solution)/shard_map/pallas_call | solution.py:293
  113.1 1.6 collective-permute-start.7
  116.2 7.5 %shard_map.77 = (f32[1,32,2560]{2,1,0:T(8,128)S(1)}, f32[1,32,2560]{2,1,0:T(8,128)S(1)}) custom-call(s32[3]{0:T(128)S(1)} %pad_add_fusion.flag_ref, bf16[3072,4608]{1,0:T(8,128)(2,1)} %counts_ref.15, f32[64,3072]{1,0:T(8,128)S(1)} %shard_map.76.refs_0_.refs_1_, f32[64,3072]{1,0:T(8,128)S(1)} %shard_map.76.refs_0_.refs_1_), custom_call_target="tpu_custom_call" | custom-call | flops 1006632960 | bytes 15597568 | tf_op jit(solution)/shard_map/pallas_call | solution.py:445
  123.8 7.3 %shard_map.78 = (f32[1,32,2304]{2,1,0:T(8,128)S(1)}, f32[1,32,2304]{2,1,0:T(8,128)S(1)}) custom-call(s32[3]{0:T(128)S(1)} %pad_add_fusion.flag_ref, bf16[3072,4608]{1,0:T(8,128)(2,1)} %counts_ref.15, f32[64,3072]{1,0:T(8,128)S(1)} %shard_map.76.refs_0_.refs_1_, f32[1,32,2560]{2,1,0:T(8,128)S(1)} %get-tuple-element.54.refs_1_.refs_0_.a), custom_call_target="tpu_custom_call" | custom-call | flops 905969664 | bytes 15532032 | tf_op jit(solution)/shard_map/pallas_call | solution.py:445
  133.7 7.5 %shard_map.82 = (f32[2,32,2560]{2,1,0:T(8,128)S(1)}, f32[2,32,2560]{2,1,0:T(8,128)S(1)}) custom-call(s32[3]{0:T(128)S(1)} %pad_add_fusion.flag_ref, bf16[3072,4608]{1,0:T(8,128)(2,1)} %counts_ref.15, f32[64,3072]{1,0:T(8,128)S(1)} %shard_map.76.refs_0_.refs_1_, f32[64,3072]{1,0:T(8,128)S(1)} %collective-permute-done.6.refs_1_, ...), custom_call_target="tpu_custom_call" | custom-call | flops 2013265920 | bytes 17825792 | tf_op jit(solution)/shard_map/pallas_call | solution.py:445
  141.6 3.2 %collective-permute-start.13 = (f32[32,2560]{1,0:T(8,128)S(1)}, f32[32,2560]{1,0:T(8,128)S(1)}, u32[]{:S(2)}, u32[]{:S(2)}) collective-permute-start(f32[32,2560]{1,0:T(8,128)S(1)} %shard_map.79.refs_2_), channel_id=1, source_target_pairs={{0,2},{1,3},{6,4},{7,5},{8,10},{9,11},{14,12},{15,13},{16,18},{17,... | collective-permute-start | bytes 983048 | tf_op jit(solution)/shard_map/ppermute | solution.py:504
  144.8 7.2 %collective-permute-done.13.refs_4_.refs_5_.refs_0_.refs_1_ = f32[32,2560]{1,0:T(8,128)S(1)} collective-permute-done((f32[32,2560]{1,0:T(8,128)S(1)}, f32[32,2560]{1,0:T(8,128)S(1)}, u32[]{:S(2)}, u32[]{:S(2)}) %collective-permute-start.13) | collective-permute-done | bytes 327712 | tf_op jit(solution)/shard_map/ppermute | solution.py:504
  152.6 7.0 %shard_map.84 = (f32[2,32,2304]{2,1,0:T(8,128)S(1)}, f32[2,32,2304]{2,1,0:T(8,128)S(1)}) custom-call(s32[3]{0:T(128)S(1)} %pad_add_fusion.flag_ref, bf16[3072,4608]{1,0:T(8,128)(2,1)} %counts_ref.15, f32[64,3072]{1,0:T(8,128)S(1)} %shard_map.76.refs_0_.refs_1_, f32[64,3072]{1,0:T(8,128)S(1)} %collective-permute-done.6.refs_1_, ...), custom_call_target="tpu_custom_call" | custom-call | flops 1811939328 | bytes 17694720 | tf_op jit(solution)/shard_map/pallas_call | solution.py:445
  159.7 4.4 %collective-permute-start.15 = (f32[32,2304]{1,0:T(8,128)S(1)}, f32[32,2304]{1,0:T(8,128)S(1)}, u32[]{:S(2)}, u32[]{:S(2)}) collective-permute-start(f32[32,2304]{1,0:T(8,128)S(1)} %shard_map.80.refs_2_), channel_id=1, source_target_pairs={{0,2},{1,3},{6,4},{7,5},{8,10},{9,11},{14,12},{15,13},{16,18},{17,... | collective-permute-start | bytes 884744 | tf_op jit(solution)/shard_map/ppermute | solution.py:504
  166.5 5.0 %collective-permute-done.15.refs_4_.refs_5_.refs_0_.refs_1_ = f32[32,2304]{1,0:T(8,128)S(1)} collective-permute-done((f32[32,2304]{1,0:T(8,128)S(1)}, f32[32,2304]{1,0:T(8,128)S(1)}, u32[]{:S(2)}, u32[]{:S(2)}) %collective-permute-start.15) | collective-permute-done | bytes 294944 | tf_op jit(solution)/shard_map/ppermute | solution.py:504
  172.7 5.0 %collective-permute-start.16 = (f32[32,2304]{1,0:T(8,128)S(1)}, f32[32,2304]{1,0:T(8,128)S(1)}, u32[]{:S(2)}, u32[]{:S(2)}) collective-permute-start(f32[32,2304]{1,0:T(8,128)S(1)} %get-tuple-element.65), channel_id=1, source_target_pairs={{0,2},{1,3},{2,4},{3,5},{8,10},{9,11},{10,12},{11,13},{16,18},{17,... | collective-permute-start | bytes 884744 | tf_op jit(solution)/shard_map/ppermute | solution.py:506
  179.8 7.5 %collective-permute-start.21 = (f32[32,2560]{1,0:T(8,128)S(1)}, f32[32,2560]{1,0:T(8,128)S(1)}, u32[]{:S(2)}, u32[]{:S(2)}) collective-permute-start(f32[32,2560]{1,0:T(8,128)S(1)} %get-tuple-element.72), channel_id=1, source_target_pairs={{0,2},{1,3},{2,4},{3,5},{4,6},{5,7},{8,10},{9,11},{10,12},{11,13},... | collective-permute-start | bytes 983048 | tf_op jit(solution)/shard_map/ppermute | solution.py:506
  189.3 7.9 %shard_map.88 = (f32[1,32,2560]{2,1,0:T(8,128)S(1)}, f32[1,32,2560]{2,1,0:T(8,128)S(1)}) custom-call(s32[3]{0:T(128)S(1)} %pad_add_fusion.flag_ref, bf16[3072,4608]{1,0:T(8,128)(2,1)} %counts_ref.15, f32[64,3072]{1,0:T(8,128)S(1)} %shard_map.76.refs_0_.refs_1_, f32[64,3072]{1,0:T(8,128)S(1)} %collective-permute-done.6.refs_1_, ...), custom_call_target="tpu_custom_call" | custom-call | flops 1006632960 | bytes 17956864 | tf_op jit(solution)/shard_map/pallas_call | solution.py:445
  198.5 5.9 %collective-permute-start.24 = (f32[32,2304]{1,0:T(8,128)S(1)}, f32[32,2304]{1,0:T(8,128)S(1)}, u32[]{:S(2)}, u32[]{:S(2)}) collective-permute-start(f32[32,2304]{1,0:T(8,128)S(1)} %get-tuple-element.76), channel_id=1, source_target_pairs={{0,2},{1,3},{2,4},{3,5},{4,6},{5,7},{8,10},{9,11},{10,12},{11,13},... | collective-permute-start | bytes 884744 | tf_op jit(solution)/shard_map/ppermute | solution.py:506
  205.1 4.0 %collective-permute-start.27 = (f32[32,2560]{1,0:T(8,128)S(1)}, f32[32,2560]{1,0:T(8,128)S(1)}, u32[]{:S(2)}, u32[]{:S(2)}) collective-permute-start(f32[32,2560]{1,0:T(8,128)S(1)} %get-tuple-element.78), channel_id=1, source_target_pairs={{0,2},{1,3},{2,4},{3,5},{4,6},{5,7},{8,10},{9,11},{10,12},{11,13},... | collective-permute-start | bytes 983048 | tf_op jit(solution)/shard_map/ppermute | solution.py:506
  210.4 7.3 %shard_map.90 = (f32[1,32,2304]{2,1,0:T(8,128)S(1)}, f32[1,32,2304]{2,1,0:T(8,128)S(1)}) custom-call(s32[3]{0:T(128)S(1)} %pad_add_fusion.flag_ref, bf16[3072,4608]{1,0:T(8,128)(2,1)} %counts_ref.15, f32[64,3072]{1,0:T(8,128)S(1)} %shard_map.76.refs_0_.refs_1_, f32[64,3072]{1,0:T(8,128)S(1)} %collective-permute-done.6.refs_1_, ...), custom_call_target="tpu_custom_call" | custom-call | flops 905969664 | bytes 17891328 | tf_op jit(solution)/shard_map/pallas_call | solution.py:445
  217.7 1.5 collective-permute-done.23.refs_5_.refs_3_.refs_1_.b
  219.9 4.2 %shard_map.92.refs_6_ = f32[3072,256]{1,0:T(8,128)} custom-call(s32[1]{0:T(128)} %bitcast.me_ref, f32[64,3072]{1,0:T(8,128)S(1)} %shard_map.76.refs_0_.refs_1_, f32[64,3072]{1,0:T(8,128)S(1)} %collective-permute-done.6.refs_1_, f32[64,3072]{1,0:T(8,128)S(1)} %collective-permute-done.7.refs_0_.refs_2_, f32[64,1536]{1,0:T(8,128)S(1)} %collective-permute-done.10.refs_3_, ...), custom_call_target="tpu_custom_call" | custom-call | bytes 6291456 | tf_op jit(solution)/shard_map/pallas_call | solution.py:383
  224.1 1.9 copy-done.1
  229.9 8.6 %collective-permute-start.29 = (f32[32,2304]{1,0:T(8,128)S(1)}, f32[32,2304]{1,0:T(8,128)S(1)}, u32[]{:S(2)}, u32[]{:S(2)}) collective-permute-start(f32[32,2304]{1,0:T(8,128)S(1)} %get-tuple-element.79), channel_id=1, source_target_pairs={{0,2},{1,3},{2,4},{3,5},{4,6},{5,7},{8,10},{9,11},{10,12},{11,13},... | collective-permute-start | bytes 884744 | tf_op jit(solution)/shard_map/ppermute | solution.py:506
  239.8 5.0 %collective-permute-done.29.refs_4_.refs_2_.refs_0_ = f32[32,2304]{1,0:T(8,128)S(1)} collective-permute-done((f32[32,2304]{1,0:T(8,128)S(1)}, f32[32,2304]{1,0:T(8,128)S(1)}, u32[]{:S(2)}, u32[]{:S(2)}) %collective-permute-start.29) | collective-permute-done | bytes 294944 | tf_op jit(solution)/shard_map/ppermute | solution.py:506
  244.7 5.8 %collective-permute-done.30.refs_5_.refs_3_.refs_1_ = f32[32,2304]{1,0:T(8,128)S(1)} collective-permute-done((f32[32,2304]{1,0:T(8,128)S(1)}, f32[32,2304]{1,0:T(8,128)S(1)}, u32[]{:S(2)}, u32[]{:S(2)}) %collective-permute-start.30) | collective-permute-done | bytes 294944 | tf_op jit(solution)/shard_map/ppermute | solution.py:506
  256.9 13.3 %collective-permute-done.35.refs_3_.refs_5_ = f32[32,2304]{1,0:T(8,128)S(1)} collective-permute-done((f32[32,2304]{1,0:T(8,128)S(1)}, f32[32,2304]{1,0:T(8,128)S(1)}, u32[]{:S(2)}, u32[]{:S(2)}) %collective-permute-start.35) | collective-permute-done | bytes 294944 | tf_op jit(solution)/shard_map/ppermute | solution.py:506
  275.2 8.8 %collective-permute-done.39.refs_4_.refs_5_ = f32[32,2304]{1,0:T(8,128)S(1)} collective-permute-done((f32[32,2304]{1,0:T(8,128)S(1)}, f32[32,2304]{1,0:T(8,128)S(1)}, u32[]{:S(2)}, u32[]{:S(2)}) %collective-permute-start.39) | collective-permute-done | bytes 294944 | tf_op jit(solution)/shard_map/ppermute | solution.py:504
  285.3 7.7 %shard_map.104.share_ref = f32[256,4608]{1,0:T(8,128)S(1)} custom-call(s32[3]{0:T(128)S(1)} %pad_add_fusion.flag_ref, f32[256,4608]{1,0:T(8,128)} %load_ref.3, f32[32,256]{1,0:T(8,128)S(1)} %slice.32.refs_0_, f32[32,256]{1,0:T(8,128)S(1)} %slice.33.refs_1_, f32[32,256]{1,0:T(8,128)S(1)} %slice.34.refs_2_, f32[32,256]{1,0:T(8,128)S(1)} %slice.35.refs_3_, ...), custom_call_target="tpu_custom_call" | custom-call | flops 3623878656 | bytes 9437184 | tf_op jit(solution)/shard_map/pallas_call | solution.py:581
  293.0 1.5 shard_map.106.rest_0_
  294.5 1.5 shard_map.107.rest_0_
  297.4 1.5 shard_map.109.rest_0_
  298.9 1.5 shard_map.110.rest_0_
  300.4 1.5 shard_map.111.rest_0_
  303.3 1.5 shard_map.113
  (110 shorter events, 42.0 us)
Async XLA Ops:
  0.6 35.4 %copy-start.4 = (s32[12,256]{1,0:T(8,128)S(1)}, s32[12,256]{1,0:T(8,128)}, u32[]{:S(2)}) copy-start(s32[12,256]{1,0:T(8,128)} %code_ref.3) | copy-start | bytes 36868
  1.4 1.9 copy-start
  6.6 29.4 %all-to-all-start = ((f32[8,72,384]{2,1,0:T(8,128)}), f32[8,72,384]{2,1,0:T(8,128)S(1)}, u32[]{:S(2)}, u32[]{:S(2)}) async-start(f32[8,72,384]{2,1,0:T(8,128)} %shard_map.68.pay_ref), calls=%async_computation | async-start | bytes 1769472 | tf_op jit(solution)/shard_map/all_to_all | solution.py:643
  38.7 13.6 %collective-permute-start = (f32[72,256]{1,0:T(8,128)S(1)}, f32[72,256]{1,0:T(8,128)S(1)}, u32[]{:S(2)}, u32[]{:S(2)}) collective-permute-start(f32[72,256]{1,0:T(8,128)S(1)} %get-tuple-element.44), channel_id=1, source_target_pairs={{0,1},{1,2},{2,3},{3,4},{4,5},{5,6},{6,7},{8,9},{9,10},{10,11},{11... | collective-permute-start | bytes 221192 | tf_op jit(solution)/shard_map/ppermute | solution.py:655
  40.3 12.1 %collective-permute-start.1 = (f32[72,256]{1,0:T(8,128)S(1)}, f32[72,256]{1,0:T(8,128)S(1)}, u32[]{:S(2)}, u32[]{:S(2)}) collective-permute-start(f32[72,256]{1,0:T(8,128)S(1)} %get-tuple-element.45), channel_id=1, source_target_pairs={{1,0},{2,1},{3,2},{4,3},{5,4},{6,5},{7,6},{9,8},{10,9},{11,10},{12... | collective-permute-start | bytes 221192 | tf_op jit(solution)/shard_map/ppermute | solution.py:656
  56.6 55.2 %all-to-all-start.1 = ((f32[8,72,384]{2,1,0:T(8,128)}), f32[8,72,384]{2,1,0:T(8,128)S(1)}, u32[]{:S(2)}, u32[]{:S(2)}) async-start(f32[8,72,384]{2,1,0:T(8,128)} %shard_map.70), calls=%async_computation.1 | async-start | bytes 1769472 | tf_op jit(solution)/shard_map/all_to_all | solution.py:658
  72.1 22.8 %collective-permute-start.2 = (f32[2,64,1792]{2,1,0:T(8,128)S(1)}, f32[2,64,1792]{2,1,0:T(8,128)S(1)}, u32[]{:S(2)}, u32[]{:S(2)}) collective-permute-start(f32[2,64,1792]{2,1,0:T(8,128)S(1)} %get-tuple-element.49), channel_id=1, source_target_pairs={{0,8},{8,0},{16,24},{24,16},{1,9},{9,1},{17,25},{25,17},{2,10},{10... | collective-permute-start | bytes 2752520 | tf_op jit(solution)/shard_map/ppermute | solution.py:225
  73.7 22.9 %collective-permute-start.4 = (f32[2,64,1536]{2,1,0:T(8,128)S(1)}, f32[2,64,1536]{2,1,0:T(8,128)S(1)}, u32[]{:S(2)}, u32[]{:S(2)}) collective-permute-start(f32[2,64,1536]{2,1,0:T(8,128)S(1)} %get-tuple-element.51), channel_id=1, source_target_pairs={{0,16},{8,24},{16,0},{24,8},{1,17},{9,25},{17,1},{25,9},{2,18},{10... | collective-permute-start | bytes 2359304 | tf_op jit(solution)/shard_map/ppermute | solution.py:225
  95.0 12.2 %collective-permute-start.3 = (f32[1,64,1792]{2,1,0:T(8,128)S(1)}, f32[1,64,1792]{2,1,0:T(8,128)S(1)}, u32[]{:S(2)}, u32[]{:S(2)}) collective-permute-start(f32[1,64,1792]{2,1,0:T(8,128)S(1)} %shard_map.73), channel_id=1, source_target_pairs={{0,16},{8,24},{16,0},{24,8},{1,17},{9,25},{17,1},{25,9},{2,18},{10... | collective-permute-start | bytes 1376264 | tf_op jit(solution)/shard_map/ppermute | solution.py:225
  96.6 10.6 %collective-permute-start.5 = (f32[1,64,1536]{2,1,0:T(8,128)S(1)}, f32[1,64,1536]{2,1,0:T(8,128)S(1)}, u32[]{:S(2)}, u32[]{:S(2)}) collective-permute-start(f32[1,64,1536]{2,1,0:T(8,128)S(1)} %shard_map.74), channel_id=1, source_target_pairs={{0,8},{8,0},{16,24},{24,16},{1,9},{9,1},{17,25},{25,17},{2,10},{10... | collective-permute-start | bytes 1179656 | tf_op jit(solution)/shard_map/ppermute | solution.py:225
  113.1 20.5 %collective-permute-start.7 = (f32[64,3072]{1,0:T(8,128)S(1)}, f32[64,3072]{1,0:T(8,128)S(1)}, u32[]{:S(2)}, u32[]{:S(2)}) collective-permute-start(f32[64,3072]{1,0:T(8,128)S(1)} %shard_map.76.refs_0_.refs_1_), channel_id=1, source_target_pairs={{0,16},{8,24},{16,0},{24,8},{1,17},{9,25},{17,1},{25,9},{2,18},{10... | collective-permute-start | bytes 2359304 | tf_op jit(solution)/shard_map/ppermute | solution.py:225
  114.7 18.9 %collective-permute-start.6 = (f32[64,3072]{1,0:T(8,128)S(1)}, f32[64,3072]{1,0:T(8,128)S(1)}, u32[]{:S(2)}, u32[]{:S(2)}) collective-permute-start(f32[64,3072]{1,0:T(8,128)S(1)} %shard_map.76.refs_0_.refs_1_), channel_id=1, source_target_pairs={{0,8},{8,0},{16,24},{24,16},{1,9},{9,1},{17,25},{25,17},{2,10},{10... | collective-permute-start | bytes 2359304 | tf_op jit(solution)/shard_map/ppermute | solution.py:225
  123.7 7.9 %collective-permute-start.9 = (f32[1,32,2560]{2,1,0:T(8,128)S(1)}, f32[1,32,2560]{2,1,0:T(8,128)S(1)}, u32[]{:S(2)}, u32[]{:S(2)}) collective-permute-start(f32[1,32,2560]{2,1,0:T(8,128)S(1)} %get-tuple-element.57), channel_id=1, source_target_pairs={{0,1},{1,0},{2,3},{3,2},{4,5},{5,4},{6,7},{7,6},{8,9},{9,8},{10,11... | collective-permute-start | bytes 983048 | tf_op jit(solution)/shard_map/ppermute | solution.py:225
  131.0 1.8 collective-permute-start.8
  141.1 10.9 %collective-permute-start.12 = (f32[2,32,2560]{2,1,0:T(8,128)S(1)}, f32[2,32,2560]{2,1,0:T(8,128)S(1)}, u32[]{:S(2)}, u32[]{:S(2)}) collective-permute-start(f32[2,32,2560]{2,1,0:T(8,128)S(1)} %get-tuple-element.61), channel_id=1, source_target_pairs={{0,1},{1,0},{2,3},{3,2},{4,5},{5,4},{6,7},{7,6},{8,9},{9,8},{10,11... | collective-permute-start | bytes 1966088 | tf_op jit(solution)/shard_map/ppermute | solution.py:225
  141.6 10.4 %collective-permute-start.13 = (f32[32,2560]{1,0:T(8,128)S(1)}, f32[32,2560]{1,0:T(8,128)S(1)}, u32[]{:S(2)}, u32[]{:S(2)}) collective-permute-start(f32[32,2560]{1,0:T(8,128)S(1)} %shard_map.79.refs_2_), channel_id=1, source_target_pairs={{0,2},{1,3},{6,4},{7,5},{8,10},{9,11},{14,12},{15,13},{16,18},{17,... | collective-permute-start | bytes 983048 | tf_op jit(solution)/shard_map/ppermute | solution.py:504
  159.7 12.5 %collective-permute-start.14 = (f32[2,32,2304]{2,1,0:T(8,128)S(1)}, f32[2,32,2304]{2,1,0:T(8,128)S(1)}, u32[]{:S(2)}, u32[]{:S(2)}) collective-permute-start(f32[2,32,2304]{2,1,0:T(8,128)S(1)} %get-tuple-element.64), channel_id=1, source_target_pairs={{0,1},{1,0},{2,3},{3,2},{4,5},{5,4},{6,7},{7,6},{8,9},{9,8},{10,11... | collective-permute-start | bytes 1769480 | tf_op jit(solution)/shard_map/ppermute | solution.py:225
  159.7 11.7 %collective-permute-start.15 = (f32[32,2304]{1,0:T(8,128)S(1)}, f32[32,2304]{1,0:T(8,128)S(1)}, u32[]{:S(2)}, u32[]{:S(2)}) collective-permute-start(f32[32,2304]{1,0:T(8,128)S(1)} %shard_map.80.refs_2_), channel_id=1, source_target_pairs={{0,2},{1,3},{6,4},{7,5},{8,10},{9,11},{14,12},{15,13},{16,18},{17,... | collective-permute-start | bytes 884744 | tf_op jit(solution)/shard_map/ppermute | solution.py:504
  164.2 14.3 %collective-permute-start.18 = (f32[32,2560]{1,0:T(8,128)S(1)}, f32[32,2560]{1,0:T(8,128)S(1)}, u32[]{:S(2)}, u32[]{:S(2)}) collective-permute-start(f32[32,2560]{1,0:T(8,128)S(1)} %get-tuple-element.67), channel_id=1, source_target_pairs={{0,2},{1,3},{2,4},{3,5},{8,10},{9,11},{10,12},{11,13},{16,18},{17,... | collective-permute-start | bytes 983048 | tf_op jit(solution)/shard_map/ppermute | solution.py:506
  165.5 23.8 %collective-permute-start.11 = (f32[64,1536]{1,0:T(8,128)S(1)}, f32[64,1536]{1,0:T(8,128)S(1)}, u32[]{:S(2)}, u32[]{:S(2)}) collective-permute-start(f32[64,1536]{1,0:T(8,128)S(1)} %get-tuple-element.59), channel_id=1, source_target_pairs={{0,16},{8,24},{16,0},{24,8},{1,17},{9,25},{17,1},{25,9},{2,18},{10... | collective-permute-start | bytes 1179656 | tf_op jit(solution)/shard_map/ppermute | solution.py:225
  166.0 23.3 %collective-permute-start.10 = (f32[64,1536]{1,0:T(8,128)S(1)}, f32[64,1536]{1,0:T(8,128)S(1)}, u32[]{:S(2)}, u32[]{:S(2)}) collective-permute-start(f32[64,1536]{1,0:T(8,128)S(1)} %get-tuple-element.58.refs_3_), channel_id=1, source_target_pairs={{0,8},{8,0},{16,24},{24,16},{1,9},{9,1},{17,25},{25,17},{2,10},{10... | collective-permute-start | bytes 1179656 | tf_op jit(solution)/shard_map/ppermute | solution.py:225
  171.4 7.7 %collective-permute-start.19 = (f32[32,2560]{1,0:T(8,128)S(1)}, f32[32,2560]{1,0:T(8,128)S(1)}, u32[]{:S(2)}, u32[]{:S(2)}) collective-permute-start(f32[32,2560]{1,0:T(8,128)S(1)} %get-tuple-element.62.refs_3_), channel_id=1, source_target_pairs={{6,4},{7,5},{4,2},{5,3},{14,12},{15,13},{12,10},{13,11},{22,20},{2... | collective-permute-start | bytes 983048 | tf_op jit(solution)/shard_map/ppermute | solution.py:506
  172.7 14.6 %collective-permute-start.16 = (f32[32,2304]{1,0:T(8,128)S(1)}, f32[32,2304]{1,0:T(8,128)S(1)}, u32[]{:S(2)}, u32[]{:S(2)}) collective-permute-start(f32[32,2304]{1,0:T(8,128)S(1)} %get-tuple-element.65), channel_id=1, source_target_pairs={{0,2},{1,3},{2,4},{3,5},{8,10},{9,11},{10,12},{11,13},{16,18},{17,... | collective-permute-start | bytes 884744 | tf_op jit(solution)/shard_map/ppermute | solution.py:506
  178.5 10.2 %collective-permute-start.17 = (f32[32,2304]{1,0:T(8,128)S(1)}, f32[32,2304]{1,0:T(8,128)S(1)}, u32[]{:S(2)}, u32[]{:S(2)}) collective-permute-start(f32[32,2304]{1,0:T(8,128)S(1)} %get-tuple-element.66.refs_8_), channel_id=1, source_target_pairs={{6,4},{7,5},{4,2},{5,3},{14,12},{15,13},{12,10},{13,11},{22,20},{2... | collective-permute-start | bytes 884744 | tf_op jit(solution)/shard_map/ppermute | solution.py:506
  179.8 24.7 %collective-permute-start.21 = (f32[32,2560]{1,0:T(8,128)S(1)}, f32[32,2560]{1,0:T(8,128)S(1)}, u32[]{:S(2)}, u32[]{:S(2)}) collective-permute-start(f32[32,2560]{1,0:T(8,128)S(1)} %get-tuple-element.72), channel_id=1, source_target_pairs={{0,2},{1,3},{2,4},{3,5},{4,6},{5,7},{8,10},{9,11},{10,12},{11,13},... | collective-permute-start | bytes 983048 | tf_op jit(solution)/shard_map/ppermute | solution.py:506
  187.3 17.1 %collective-permute-start.22 = (f32[32,2560]{1,0:T(8,128)S(1)}, f32[32,2560]{1,0:T(8,128)S(1)}, u32[]{:S(2)}, u32[]{:S(2)}) collective-permute-start(f32[32,2560]{1,0:T(8,128)S(1)} %get-tuple-element.68.refs_8_), channel_id=1, source_target_pairs={{6,4},{7,5},{4,2},{5,3},{2,0},{3,1},{14,12},{15,13},{12,10},{13,11... | collective-permute-start | bytes 983048 | tf_op jit(solution)/shard_map/ppermute | solution.py:506
  197.1 7.3 %collective-permute-start.20 = (f32[1,32,2560]{2,1,0:T(8,128)S(1)}, f32[1,32,2560]{2,1,0:T(8,128)S(1)}, u32[]{:S(2)}, u32[]{:S(2)}) collective-permute-start(f32[1,32,2560]{2,1,0:T(8,128)S(1)} %get-tuple-element.71), channel_id=1, source_target_pairs={{0,1},{1,0},{2,3},{3,2},{4,5},{5,4},{6,7},{7,6},{8,9},{9,8},{10,11... | collective-permute-start | bytes 983048 | tf_op jit(solution)/shard_map/ppermute | solution.py:225
  197.2 20.5 %collective-permute-start.25 = (f32[32,2304]{1,0:T(8,128)S(1)}, f32[32,2304]{1,0:T(8,128)S(1)}, u32[]{:S(2)}, u32[]{:S(2)}) collective-permute-start(f32[32,2304]{1,0:T(8,128)S(1)} %get-tuple-element.69.refs_5_), channel_id=1, source_target_pairs={{6,4},{7,5},{4,2},{5,3},{2,0},{3,1},{14,12},{15,13},{12,10},{13,11... | collective-permute-start | bytes 884744 | tf_op jit(solution)/shard_map/ppermute | solution.py:506
  198.5 19.2 %collective-permute-start.24 = (f32[32,2304]{1,0:T(8,128)S(1)}, f32[32,2304]{1,0:T(8,128)S(1)}, u32[]{:S(2)}, u32[]{:S(2)}) collective-permute-start(f32[32,2304]{1,0:T(8,128)S(1)} %get-tuple-element.76), channel_id=1, source_target_pairs={{0,2},{1,3},{2,4},{3,5},{4,6},{5,7},{8,10},{9,11},{10,12},{11,13},... | collective-permute-start | bytes 884744 | tf_op jit(solution)/shard_map/ppermute | solution.py:506
  205.1 22.2 %collective-permute-start.27 = (f32[32,2560]{1,0:T(8,128)S(1)}, f32[32,2560]{1,0:T(8,128)S(1)}, u32[]{:S(2)}, u32[]{:S(2)}) collective-permute-start(f32[32,2560]{1,0:T(8,128)S(1)} %get-tuple-element.78), channel_id=1, source_target_pairs={{0,2},{1,3},{2,4},{3,5},{4,6},{5,7},{8,10},{9,11},{10,12},{11,13},... | collective-permute-start | bytes 983048 | tf_op jit(solution)/shard_map/ppermute | solution.py:506
  209.1 18.2 %collective-permute-start.28 = (f32[32,2560]{1,0:T(8,128)S(1)}, f32[32,2560]{1,0:T(8,128)S(1)}, u32[]{:S(2)}, u32[]{:S(2)}) collective-permute-start(f32[32,2560]{1,0:T(8,128)S(1)} %get-tuple-element.73.refs_5_), channel_id=1, source_target_pairs={{6,4},{7,5},{4,2},{5,3},{2,0},{3,1},{14,12},{15,13},{12,10},{13,11... | collective-permute-start | bytes 983048 | tf_op jit(solution)/shard_map/ppermute | solution.py:506
  217.6 1.6 collective-permute-start.23
  227.9 24.5 %collective-permute-start.32 = (f32[32,2560]{1,0:T(8,128)S(1)}, f32[32,2560]{1,0:T(8,128)S(1)}, u32[]{:S(2)}, u32[]{:S(2)}) collective-permute-start(f32[32,2560]{1,0:T(8,128)S(1)} %get-tuple-element.82), channel_id=1, source_target_pairs={{2,4},{3,5},{4,6},{5,7},{10,12},{11,13},{12,14},{13,15},{18,20},{1... | collective-permute-start | bytes 983048 | tf_op jit(solution)/shard_map/ppermute | solution.py:506
  228.6 23.9 %collective-permute-start.33 = (f32[32,2560]{1,0:T(8,128)S(1)}, f32[32,2560]{1,0:T(8,128)S(1)}, u32[]{:S(2)}, u32[]{:S(2)}) collective-permute-start(f32[32,2560]{1,0:T(8,128)S(1)} %get-tuple-element.80.refs_6_), channel_id=1, source_target_pairs={{4,2},{5,3},{2,0},{3,1},{12,10},{13,11},{10,8},{11,9},{20,18},{21,... | collective-permute-start | bytes 983048 | tf_op jit(solution)/shard_map/ppermute | solution.py:506
  229.9 14.9 %collective-permute-start.29 = (f32[32,2304]{1,0:T(8,128)S(1)}, f32[32,2304]{1,0:T(8,128)S(1)}, u32[]{:S(2)}, u32[]{:S(2)}) collective-permute-start(f32[32,2304]{1,0:T(8,128)S(1)} %get-tuple-element.79), channel_id=1, source_target_pairs={{0,2},{1,3},{2,4},{3,5},{4,6},{5,7},{8,10},{9,11},{10,12},{11,13},... | collective-permute-start | bytes 884744 | tf_op jit(solution)/shard_map/ppermute | solution.py:506
  238.5 12.1 %collective-permute-start.30 = (f32[32,2304]{1,0:T(8,128)S(1)}, f32[32,2304]{1,0:T(8,128)S(1)}, u32[]{:S(2)}, u32[]{:S(2)}) collective-permute-start(f32[32,2304]{1,0:T(8,128)S(1)} %get-tuple-element.77.refs_5_), channel_id=1, source_target_pairs={{6,4},{7,5},{4,2},{5,3},{2,0},{3,1},{14,12},{15,13},{12,10},{13,11... | collective-permute-start | bytes 884744 | tf_op jit(solution)/shard_map/ppermute | solution.py:506
  253.0 19.0 %collective-permute-start.37 = (f32[32,2560]{1,0:T(8,128)S(1)}, f32[32,2560]{1,0:T(8,128)S(1)}, u32[]{:S(2)}, u32[]{:S(2)}) collective-permute-start(f32[32,2560]{1,0:T(8,128)S(1)} %shard_map.99.refs_4_), channel_id=1, source_target_pairs={{4,6},{5,7},{2,0},{3,1},{12,14},{13,15},{10,8},{11,9},{20,22},{21,... | collective-permute-start | bytes 983048 | tf_op jit(solution)/shard_map/ppermute | solution.py:504
  254.3 2.6 collective-permute-start.34
  255.0 15.2 %collective-permute-start.35 = (f32[32,2304]{1,0:T(8,128)S(1)}, f32[32,2304]{1,0:T(8,128)S(1)}, u32[]{:S(2)}, u32[]{:S(2)}) collective-permute-start(f32[32,2304]{1,0:T(8,128)S(1)} %get-tuple-element.81.refs_6_), channel_id=1, source_target_pairs={{4,2},{5,3},{2,0},{3,1},{12,10},{13,11},{10,8},{11,9},{20,18},{21,... | collective-permute-start | bytes 884744 | tf_op jit(solution)/shard_map/ppermute | solution.py:506
  256.3 18.3 %collective-permute-start.26 = (f32[32,2560]{1,0:T(8,128)S(1)}, f32[32,2560]{1,0:T(8,128)S(1)}, u32[]{:S(2)}, u32[]{:S(2)}) collective-permute-start(f32[32,2560]{1,0:T(8,128)S(1)} %shard_map.93.refs_6_.mine_ref), channel_id=1, source_target_pairs={{0,1},{1,0},{2,3},{3,2},{4,5},{5,4},{6,7},{7,6},{8,9},{9,8},{10,11... | collective-permute-start | bytes 983048 | tf_op jit(solution)/shard_map/ppermute | solution.py:225
  256.4 18.3 %collective-permute-start.31 = (f32[32,2560]{1,0:T(8,128)S(1)}, f32[32,2560]{1,0:T(8,128)S(1)}, u32[]{:S(2)}, u32[]{:S(2)}) collective-permute-start(f32[32,2560]{1,0:T(8,128)S(1)} %shard_map.97.refs_6_.mine_ref), channel_id=1, source_target_pairs={{0,1},{1,0},{2,3},{3,2},{4,5},{5,4},{6,7},{7,6},{8,9},{9,8},{10,11... | collective-permute-start | bytes 983048 | tf_op jit(solution)/shard_map/ppermute | solution.py:225
  271.3 13.4 %collective-permute-start.36 = (f32[32,2560]{1,0:T(8,128)S(1)}, f32[32,2560]{1,0:T(8,128)S(1)}, u32[]{:S(2)}, u32[]{:S(2)}) collective-permute-start(f32[32,2560]{1,0:T(8,128)S(1)} %shard_map.101.refs_6_.mine_ref), channel_id=1, source_target_pairs={{0,1},{1,0},{2,3},{3,2},{4,5},{5,4},{6,7},{7,6},{8,9},{9,8},{10,11... | collective-permute-start | bytes 983048 | tf_op jit(solution)/shard_map/ppermute | solution.py:225
  272.7 12.6 %collective-permute-start.38 = (f32[32,2560]{1,0:T(8,128)S(1)}, f32[32,2560]{1,0:T(8,128)S(1)}, u32[]{:S(2)}, u32[]{:S(2)}) collective-permute-start(f32[32,2560]{1,0:T(8,128)S(1)} %shard_map.103.refs_6_.mine_ref), channel_id=1, source_target_pairs={{0,1},{1,0},{2,3},{3,2},{4,5},{5,4},{6,7},{7,6},{8,9},{9,8},{10,11... | collective-permute-start | bytes 983048 | tf_op jit(solution)/shard_map/ppermute | solution.py:225
  273.2 10.8 %collective-permute-start.39 = (f32[32,2304]{1,0:T(8,128)S(1)}, f32[32,2304]{1,0:T(8,128)S(1)}, u32[]{:S(2)}, u32[]{:S(2)}) collective-permute-start(f32[32,2304]{1,0:T(8,128)S(1)} %shard_map.100.refs_6_), channel_id=1, source_target_pairs={{4,6},{5,7},{2,0},{3,1},{12,14},{13,15},{10,8},{11,9},{20,22},{21,... | collective-permute-start | bytes 884744 | tf_op jit(solution)/shard_map/ppermute | solution.py:504
  274.6 19.9 %collective-permute-start.43 = (f32[32,2304]{1,0:T(8,128)S(1)}, f32[32,2304]{1,0:T(8,128)S(1)}, u32[]{:S(2)}, u32[]{:S(2)}) collective-permute-start(f32[32,2304]{1,0:T(8,128)S(1)} %shard_map.94.refs_6_.mine_ref), channel_id=1, source_target_pairs={{0,1},{1,0},{2,3},{3,2},{4,5},{5,4},{6,7},{7,6},{8,9},{9,8},{10,11... | collective-permute-start | bytes 884744 | tf_op jit(solution)/shard_map/ppermute | solution.py:225
  274.7 22.8 %collective-permute-start.42 = (f32[32,2304]{1,0:T(8,128)S(1)}, f32[32,2304]{1,0:T(8,128)S(1)}, u32[]{:S(2)}, u32[]{:S(2)}) collective-permute-start(f32[32,2304]{1,0:T(8,128)S(1)} %shard_map.98.refs_4_.mine_ref), channel_id=1, source_target_pairs={{0,1},{1,0},{2,3},{3,2},{4,5},{5,4},{6,7},{7,6},{8,9},{9,8},{10,11... | collective-permute-start | bytes 884744 | tf_op jit(solution)/shard_map/ppermute | solution.py:225
  284.1 16.3 %collective-permute-start.41 = (f32[32,2304]{1,0:T(8,128)S(1)}, f32[32,2304]{1,0:T(8,128)S(1)}, u32[]{:S(2)}, u32[]{:S(2)}) collective-permute-start(f32[32,2304]{1,0:T(8,128)S(1)} %shard_map.102.refs_6_.mine_ref), channel_id=1, source_target_pairs={{0,1},{1,0},{2,3},{3,2},{4,5},{5,4},{6,7},{7,6},{8,9},{9,8},{10,11... | collective-permute-start | bytes 884744 | tf_op jit(solution)/shard_map/ppermute | solution.py:225
  284.7 18.6 %collective-permute-start.40 = (f32[32,2304]{1,0:T(8,128)S(1)}, f32[32,2304]{1,0:T(8,128)S(1)}, u32[]{:S(2)}, u32[]{:S(2)}) collective-permute-start(f32[32,2304]{1,0:T(8,128)S(1)} %shard_map.105.mine_ref), channel_id=1, source_target_pairs={{0,1},{1,0},{2,3},{3,2},{4,5},{5,4},{6,7},{7,6},{8,9},{9,8},{10,11... | collective-permute-start | bytes 884744 | tf_op jit(solution)/shard_map/ppermute | solution.py:225
  (3 other events, 5.0 us)
